TPU v7x, 256 devices: a whole 4x4x8 slice. The times are simulated.
256 devices in a mesh: adapter: 16 (over x_lo, y, core), tensor: 16 (over x_hi, z).
Axes of the slice: x: 4 (x_hi: 2, x_lo: 2; x = x_hi * 2 + x_lo), y: 4, z: 8, core: 2. Of those that a mesh axis runs over, the one named last changes fastest.
Arguments:
- tokens: bfloat16 [8192, 8192], P('adapter', 'tensor'), may hold values from -6 to 6
- cotangent: bfloat16 [8192, 8192], P('adapter', 'tensor'), may hold values from -1.5 to 1.5
- frozen_weight: bfloat16 [8192, 8192], P('adapter', 'tensor'), may hold values from -0.0625 to 0.0625
- adapter_per_tile: int32 [16, 4], P('adapter'), may hold values from 0 to 63, as said below
- tile_token_length: int32 [16, 4], P('adapter'), may hold values from 1 to 128, as said below
- adapter_down_weight: float32 [64, 64, 8192], P('adapter', None, 'tensor'), may hold values from -0.0625 to 0.0625
- adapter_up_weight: float32 [64, 64, 8192], P('adapter', None, 'tensor'), may hold values from -0.1875 to 0.1875
- down_first_moment: float32 [64, 64, 8192], P('adapter', None, 'tensor'), may hold values from -18 to 18
- down_second_moment: float32 [64, 64, 8192], P('adapter', None, 'tensor'), may hold values from 0.03 to 0.3
- up_first_moment: float32 [64, 64, 8192], P('adapter', None, 'tensor'), may hold values from -6 to 6
- up_second_moment: float32 [64, 64, 8192], P('adapter', None, 'tensor'), may hold values from 0.003 to 0.03
Outputs:
- output: bfloat16 [8192, 8192], P('adapter', 'tensor')
- token_gradient: bfloat16 [8192, 8192], P('adapter', 'tensor')
- fresh_down_weight: float32 [64, 64, 8192], P('adapter', None, 'tensor')
- fresh_up_weight: float32 [64, 64, 8192], P('adapter', None, 'tensor')
- fresh_down_first_moment: float32 [64, 64, 8192], P('adapter', None, 'tensor')
- fresh_down_second_moment: float32 [64, 64, 8192], P('adapter', None, 'tensor')
- fresh_up_first_moment: float32 [64, 64, 8192], P('adapter', None, 'tensor')
- fresh_up_second_moment: float32 [64, 64, 8192], P('adapter', None, 'tensor')
Inputs may be any that keep to these rules, and one draw needn't show every extreme that they name: `adapter_per_tile`: adapter k * 4 + j belongs to owner k. The 4 tiles of one batch shard belong to adapters of 4 different owners; in every draw some owner has a tile from every batch shard. `tile_token_length`: the first tile of every batch shard is full.
All inputs are finite; a program needn't handle non-finite values.
Results may differ from a plain program's by a relative error of at most 0.02.
Values may be sent and summed in bfloat16 or wider, within the bound.
No kernel may reach another device: no remote copies, remote signals or barrier semaphores. Data moves between devices by JAX's collectives and lax.ppermute only.
A program may use at most 128 MiB of HBM per device.

v0:
```python
import jax
import jax.numpy as jnp
from jax import lax
from jax.sharding import PartitionSpec as P

ADAM_STEP = 10


adapter_scale = 0.5
beta_one = 0.9
beta_two = 0.999
adam_eps = 1e-08
weight_decay = 0.01
learn_rate = 0.001


def decoupled_adam(parameter, moment, second, gradient):
    moment_new = beta_one * moment + (1.0 - beta_one) * gradient
    second_new = beta_two * second + (1.0 - beta_two) * gradient * gradient
    bias_first = 1.0 - beta_one**ADAM_STEP
    bias_second = 1.0 - beta_two**ADAM_STEP
    update = (
        moment_new / bias_first / (jnp.sqrt(second_new / bias_second) + adam_eps)
        + weight_decay * parameter
    )
    return (parameter - learn_rate * update, moment_new, second_new)


def masked_down(row_block, weights, slot_ids, indicator_matrix):
    count, height, width = row_block.shape
    held, low_rank, _ = weights.shape
    products = lax.dot_general(
        row_block.reshape(count * height, width),
        weights.reshape(held * low_rank, width),
        (((1,), (1,)), ((), ())),
        preferred_element_type=jnp.float32,
    )
    products = products.reshape(count, height, held, low_rank)
    return jnp.sum(products * indicator_matrix[:, None, :, None], axis=2)


def masked_spread(low_rows, indicator_matrix):
    count, height, low_rank = low_rows.shape
    held = indicator_matrix.shape[1]
    spread = low_rows[:, :, None, :] * indicator_matrix.astype(jnp.bfloat16)[:, None, :, None]
    return spread.reshape(count * height, held * low_rank)


def masked_up(low_rows, weights, slot_ids, indicator_matrix):
    count, height, _ = low_rows.shape
    held, low_rank, width = weights.shape
    spread = masked_spread(low_rows, indicator_matrix)
    return jnp.dot(
        spread, weights.reshape(held * low_rank, width), preferred_element_type=jnp.float32
    ).reshape(count, height, width)


def masked_outer(low_rows, row_block, slot_ids, indicator_matrix):
    count, height, width = row_block.shape
    held = indicator_matrix.shape[1]
    low_rank = low_rows.shape[2]
    spread = masked_spread(low_rows, indicator_matrix)
    outer = lax.dot_general(
        spread,
        row_block.reshape(count * height, width),
        (((0,), (0,)), ((), ())),
        preferred_element_type=jnp.float32,
    )
    return outer.reshape(held, low_rank, width)


def per_device(
    tokens,
    cotangent,
    frozen_weight,
    adapter_per_tile,
    tile_token_length,
    adapter_down_weight,
    adapter_up_weight,
    down_first_moment,
    down_second_moment,
    up_first_moment,
    up_second_moment,
):
    owners = lax.axis_size("adapter")
    tok_rows, width_local = tokens.shape
    tile_count = adapter_per_tile.shape[1]
    tile_rows = tok_rows // tile_count
    owner_grouping = adapter_down_weight.shape[0]
    adapters_here = adapter_per_tile[0]
    tile_len = tile_token_length[0]
    position = jnp.arange(tile_rows, dtype=jnp.int32)
    kept_rows = position[None, :] < tile_len[:, None]
    x_tiles = tokens.reshape(tile_count, tile_rows, width_local)
    dy_tiles = jnp.where(
        kept_rows[:, :, None],
        cotangent.reshape(tile_count, tile_rows, width_local),
        jnp.zeros((), jnp.bfloat16),
    )
    dy_flat = dy_tiles.reshape(tok_rows, width_local)
    owner_of = adapters_here // owner_grouping
    select = owner_of[None, :] == jnp.arange(owners, dtype=jnp.int32)[:, None]
    select_half = select.astype(jnp.bfloat16)
    send_x = jnp.einsum(
        "ot,tkf->okf", select_half, x_tiles, preferred_element_type=jnp.float32
    ).astype(jnp.bfloat16)
    send_dy = jnp.einsum(
        "ot,tkf->okf", select_half, dy_tiles, preferred_element_type=jnp.float32
    ).astype(jnp.bfloat16)
    local_slot = jnp.sum(jnp.where(select, adapters_here[None, :] % owner_grouping, 0), axis=1)
    slot_ids = local_slot + jnp.where(jnp.any(select, axis=1), 0, owner_grouping)
    weight_cols = lax.all_gather(frozen_weight, "adapter", axis=0, tiled=True)
    frozen_output = jnp.dot(
        lax.all_gather(tokens, "tensor", axis=1, tiled=True),
        weight_cols,
        preferred_element_type=jnp.float32,
    )
    down_portion = adapter_down_weight.astype(jnp.bfloat16)
    up_portion = adapter_up_weight.astype(jnp.bfloat16)
    apply_down, up_projection_apply, outer_product_apply = (masked_down, masked_up, masked_outer)
    arrived_input, arrived_output_gradient, arrived_adapter_index = (
        lax.all_to_all(send_x, "adapter", split_axis=0, concat_axis=0, tiled=True),
        lax.all_to_all(send_dy, "adapter", split_axis=0, concat_axis=0, tiled=True),
        lax.all_to_all(slot_ids, "adapter", split_axis=0, concat_axis=0, tiled=True),
    )
    indicator_matrix = (
        arrived_adapter_index[:, None] == jnp.arange(owner_grouping, dtype=jnp.int32)[None, :]
    ).astype(jnp.float32)
    fwd_sum, bwd_sum = (
        lax.psum(
            apply_down(arrived_input, down_portion, arrived_adapter_index, indicator_matrix).astype(
                jnp.bfloat16
            ),
            "tensor",
        ).astype(jnp.float32),
        lax.psum(
            apply_down(
                arrived_output_gradient, up_portion, arrived_adapter_index, indicator_matrix
            ).astype(jnp.bfloat16),
            "tensor",
        ).astype(jnp.float32),
    )
    narrow_forward_pass = fwd_sum.astype(jnp.bfloat16)
    narrow_backward_pass = bwd_sum.astype(jnp.bfloat16)
    adapter_output = (
        adapter_scale
        * up_projection_apply(
            narrow_forward_pass, up_portion, arrived_adapter_index, indicator_matrix
        )
    ).astype(jnp.bfloat16)
    adapter_gradient = (
        adapter_scale
        * up_projection_apply(
            narrow_backward_pass, down_portion, arrived_adapter_index, indicator_matrix
        )
    ).astype(jnp.bfloat16)
    back_out, back_grad = (
        lax.all_to_all(adapter_output, "adapter", split_axis=0, concat_axis=0, tiled=True),
        lax.all_to_all(adapter_gradient, "adapter", split_axis=0, concat_axis=0, tiled=True),
    )
    up_gradient = adapter_scale * outer_product_apply(
        narrow_forward_pass, arrived_output_gradient, arrived_adapter_index, indicator_matrix
    )
    down_gradient = adapter_scale * outer_product_apply(
        narrow_backward_pass, arrived_input, arrived_adapter_index, indicator_matrix
    )
    mine_out = jnp.einsum(
        "ot,okf->tkf", select_half, back_out, preferred_element_type=jnp.float32
    ).reshape(tok_rows, width_local)
    mine_grad = jnp.einsum(
        "ot,okf->tkf", select_half, back_grad, preferred_element_type=jnp.float32
    ).reshape(tok_rows, width_local)
    output = (frozen_output + mine_out).astype(jnp.bfloat16)
    input_terms = lax.dot_general(
        dy_flat, weight_cols, (((1,), (1,)), ((), ())), preferred_element_type=jnp.float32
    )
    input_sum = lax.psum_scatter(
        input_terms.astype(jnp.bfloat16), "tensor", scatter_dimension=1, tiled=True
    ).astype(jnp.float32)
    token_gradient = (input_sum + mine_grad).astype(jnp.bfloat16)
    fresh_down_weight, fresh_down_first_moment, fresh_down_second_moment = decoupled_adam(
        adapter_down_weight, down_first_moment, down_second_moment, down_gradient
    )
    fresh_up_weight, fresh_up_first_moment, fresh_up_second_moment = decoupled_adam(
        adapter_up_weight, up_first_moment, up_second_moment, up_gradient
    )
    return (
        output,
        token_gradient,
        fresh_down_weight,
        fresh_up_weight,
        fresh_down_first_moment,
        fresh_down_second_moment,
        fresh_up_first_moment,
        fresh_up_second_moment,
    )


def solution(mesh):
    return jax.shard_map(
        per_device,
        mesh=mesh,
        in_specs=(
            P("adapter", "tensor"),
            P("adapter", "tensor"),
            P("adapter", "tensor"),
            P("adapter", None),
            P("adapter", None),
            P("adapter", None, "tensor"),
            P("adapter", None, "tensor"),
            P("adapter", None, "tensor"),
            P("adapter", None, "tensor"),
            P("adapter", None, "tensor"),
            P("adapter", None, "tensor"),
        ),
        out_specs=(
            P("adapter", "tensor"),
            P("adapter", "tensor"),
            P("adapter", None, "tensor"),
            P("adapter", None, "tensor"),
            P("adapter", None, "tensor"),
            P("adapter", None, "tensor"),
            P("adapter", None, "tensor"),
            P("adapter", None, "tensor"),
        ),
        check_vma=False,
    )
```

profile of v0, /device:TPU:1, one launch (start us, length us, event | category | flops | bytes accessed | tf_op | source)
XLA Modules:
  0.0 542.9 jit_solution(11084416033019762124)
XLA Ops:
  10.3 6.9 %all-to-all-start.1 = ((s32[16,1,1]{2,1,0:T(1,128)}), s32[16,1,1]{2,1,0:T(1,128)S(1)}, u32[]{:S(2)}, u32[]{:S(2)}) async-start(s32[16,1,1]{2,1,0:T(1,128)} %copy.53), calls=%async_computation.1 | async-start | bytes 16384 | tf_op jit(solution)/shard_map/all_to_all | solution.py:124
  19.1 2.5 copy.52
  22.6 4.9 all-to-all-start
  28.8 2.6 copy.62
  31.4 40.4 %all-to-all-done = bf16[16,128,512]{2,1,0:T(8,128)(2,1)S(1)} async-done(((bf16[16,128,512]{2,1,0:T(8,128)(2,1)}), bf16[16,128,512]{2,1,0:T(8,128)(2,1)S(1)}, u32[]{:S(2)}, u32[]{:S(2)}) %all-to-all-start) | async-done | bytes 2097184 | tf_op jit(solution)/shard_map/all_to_all | solution.py:122
  71.8 5.2 all-to-all-start.3
  79.0 35.9 %all-to-all-done.3 = bf16[16,128,512]{2,1,0:T(8,128)(2,1)} async-done(((bf16[16,128,512]{2,1,0:T(8,128)(2,1)}), bf16[16,128,512]{2,1,0:T(8,128)(2,1)}, u32[]{:S(2)}, u32[]{:S(2)}) %all-to-all-start.3) | async-done | bytes 2097184 | tf_op jit(solution)/shard_map/all_to_all | solution.py:123
  114.9 3.2 multiply_reduce_fusion
  119.1 10.3 %convolution_convert_fusion = bf16[512,8192]{1,0:T(8,128)(2,1)} fusion(bf16[8192,512]{1,0:T(8,128)(2,1)} %all-gather.5.cloned.1.call-done, bf16[512,512]{1,0:T(8,128)(2,1)S(1)} %copy-done.2, pred[512]{0:T(512)(128)(4,1)S(1)} %get-tuple-element.18), kind=kOutput, calls=%fused_computation | convolution fusion | flops 4299423744 | bytes 17302016 | tf_op jit(solution)/shard_map/dot_general | solution.py:174
  129.5 163.0 %all-reduce.3.cloned.1.call-done = (bf16[16,128,64]{1,2,0:T(8,128)(2,1)}, bf16[16,128,64]{1,2,0:T(8,128)(2,1)}) async-done(((bf16[16,128,64]{1,2,0:T(8,128)(2,1)}, bf16[16,128,64]{1,2,0:T(8,128)(2,1)}), (bf16[16,128,64]{1,2,0:T(8,128)(2,1)}, bf16[16,128,64]{1,2,0:T(8,128)(2,1)})) %all-reduce.3.cloned.1.call-update) | async-done | bytes 524304 | tf_op jit(solution)/shard_map/psum | solution.py:130
  295.1 4.2 copy.56
  301.7 2.5 copy.57
  304.1 14.8 %all-to-all-start.2 = ((bf16[16,128,512]{2,1,0:T(8,128)(2,1)}), bf16[16,128,512]{2,1,0:T(8,128)(2,1)}, u32[]{:S(2)}, u32[]{:S(2)}) async-start(bf16[16,128,512]{2,1,0:T(8,128)(2,1)} %copy.57), calls=%async_computation.2 | async-start | bytes 4194304 | tf_op jit(solution)/shard_map/all_to_all | solution.py:158
  319.0 4.2 copy.64
  323.2 2.4 fusion
  325.6 2.5 copy.65
  328.0 20.7 %all-to-all-done.2 = bf16[16,128,512]{2,1,0:T(8,128)(2,1)} async-done(((bf16[16,128,512]{2,1,0:T(8,128)(2,1)}), bf16[16,128,512]{2,1,0:T(8,128)(2,1)}, u32[]{:S(2)}, u32[]{:S(2)}) %all-to-all-start.2) | async-done | bytes 2097184 | tf_op jit(solution)/shard_map/all_to_all | solution.py:158
  348.7 7.4 %all-to-all-start.4 = ((bf16[16,128,512]{2,1,0:T(8,128)(2,1)}), bf16[16,128,512]{2,1,0:T(8,128)(2,1)}, u32[]{:S(2)}, u32[]{:S(2)}) async-start(bf16[16,128,512]{2,1,0:T(8,128)(2,1)} %copy.65), calls=%async_computation.5 | async-start | bytes 4194304 | tf_op jit(solution)/shard_map/all_to_all | solution.py:159
  360.2 3.8 multiply_subtract_fusion
  364.0 2.9 fusion.8
  367.3 20.8 %all-to-all-done.4 = bf16[16,128,512]{2,1,0:T(8,128)(2,1)} async-done(((bf16[16,128,512]{2,1,0:T(8,128)(2,1)}), bf16[16,128,512]{2,1,0:T(8,128)(2,1)}, u32[]{:S(2)}, u32[]{:S(2)}) %all-to-all-start.4) | async-done | bytes 2097184 | tf_op jit(solution)/shard_map/all_to_all | solution.py:159
  388.1 2.9 fusion.6
  391.4 11.1 %fusion.14 = bf16[512,512]{1,0:T(8,128)(2,1)} fusion(f32[512,512]{1,0:T(8,128)S(1)} %bitcast.95, bf16[512,8192]{1,0:T(8,128)(2,1)} %all-gather.3.cloned.1.call-done, bf16[8192,512]{1,0:T(8,128)(2,1)} %all-gather.5.cloned.1.call-done), kind=kOutput, calls=%fused_computation.18 | convolution fusion | flops 4295491584 | bytes 18350080 | tf_op jit(solution)/shard_map/dot_general | solution.py:113
  402.5 130.9 %reduce-scatter.2.cloned.1.call-done = bf16[512,512]{1,0:T(8,128)(2,1)} async-done(((bf16[512,8192]{1,0:T(8,128)(2,1)}), bf16[512,512]{1,0:T(8,128)(2,1)}) %reduce-scatter.2.cloned.1.call-update) | async-done | bytes 524304 | tf_op jit(solution)/shard_map/reduce_scatter | solution.py:177
  (56 shorter events, 21.2 us)
Async XLA Ops:
  8.0 111.1 %all-gather.5.cloned.1.call-start = ((), (), s32[]{:S(2)}) async-start(), calls=%async_computation.7 | async-start | bytes 8912896 | tf_op jit(solution)/shard_map/all_gather | solution.py:112
  10.3 12.3 %all-to-all-start.1 = ((s32[16,1,1]{2,1,0:T(1,128)}), s32[16,1,1]{2,1,0:T(1,128)S(1)}, u32[]{:S(2)}, u32[]{:S(2)}) async-start(s32[16,1,1]{2,1,0:T(1,128)} %copy.53), calls=%async_computation.1 | async-start | bytes 16384 | tf_op jit(solution)/shard_map/all_to_all | solution.py:124
  21.6 5.9 %copy-start.10 = (s32[1,4]{1,0:T(1,128)S(1)}, s32[1,4]{1,0:T(1,128)}, u32[]{:S(2)}) copy-start(s32[1,4]{1,0:T(1,128)} %param.15) | copy-start | bytes 52
  21.6 6.1 %copy-start.2 = (bf16[512,512]{1,0:T(8,128)(2,1)S(1)}, bf16[512,512]{1,0:T(8,128)(2,1)}, u32[]{:S(2)}) copy-start(bf16[512,512]{1,0:T(8,128)(2,1)} %param.12) | copy-start | bytes 1572868
  22.6 49.2 %all-to-all-start = ((bf16[16,128,512]{2,1,0:T(8,128)(2,1)}), bf16[16,128,512]{2,1,0:T(8,128)(2,1)S(1)}, u32[]{:S(2)}, u32[]{:S(2)}) async-start(bf16[16,128,512]{2,1,0:T(8,128)(2,1)} %copy.52), calls=%async_computation | async-start | bytes 4194304 | tf_op jit(solution)/shard_map/all_to_all | solution.py:122
  31.4 46.1 %copy-start.3 = (f32[4,64,512]{2,1,0:T(8,128)S(1)}, f32[4,64,512]{2,1,0:T(8,128)}, u32[]{:S(2)}) copy-start(f32[4,64,512]{2,1,0:T(8,128)} %param.16) | copy-start | bytes 1572868
  71.8 5.7 %copy-start = (bf16[16,128,512]{2,1,0:T(8,128)(2,1)}, bf16[16,128,512]{2,1,0:T(8,128)(2,1)S(1)}, u32[]{:S(2)}) copy-start(bf16[16,128,512]{2,1,0:T(8,128)(2,1)S(1)} %all-to-all-done) | copy-start | bytes 6291460
  71.8 43.1 %all-to-all-start.3 = ((bf16[16,128,512]{2,1,0:T(8,128)(2,1)}), bf16[16,128,512]{2,1,0:T(8,128)(2,1)}, u32[]{:S(2)}, u32[]{:S(2)}) async-start(bf16[16,128,512]{2,1,0:T(8,128)(2,1)} %copy.62), calls=%async_computation.4 | async-start | bytes 4194304 | tf_op jit(solution)/shard_map/all_to_all | solution.py:123
  77.0 215.5 %all-reduce.3.cloned.1.call-start = ((), (), s32[]{:S(2)}) async-start(), calls=%async_computation.9 | async-start | bytes 1048576 | tf_op jit(solution)/shard_map/psum | solution.py:130
  118.1 273.3 %all-gather.3.cloned.1.call-start = ((), (), s32[]{:S(2)}) async-start(), calls=%async_computation.6 | async-start | bytes 8912896 | tf_op jit(solution)/shard_map/all_gather | solution.py:114
  118.9 414.5 %reduce-scatter.2.cloned.1.call-start = ((), (), s32[]{:S(2)}) async-start(), calls=%async_computation.8 | async-start | bytes 8912896 | tf_op jit(solution)/shard_map/reduce_scatter | solution.py:177
  295.0 4.2 copy-start.6
  304.1 44.6 %all-to-all-start.2 = ((bf16[16,128,512]{2,1,0:T(8,128)(2,1)}), bf16[16,128,512]{2,1,0:T(8,128)(2,1)}, u32[]{:S(2)}, u32[]{:S(2)}) async-start(bf16[16,128,512]{2,1,0:T(8,128)(2,1)} %copy.57), calls=%async_computation.2 | async-start | bytes 4194304 | tf_op jit(solution)/shard_map/all_to_all | solution.py:158
  348.7 39.4 %all-to-all-start.4 = ((bf16[16,128,512]{2,1,0:T(8,128)(2,1)}), bf16[16,128,512]{2,1,0:T(8,128)(2,1)}, u32[]{:S(2)}, u32[]{:S(2)}) async-start(bf16[16,128,512]{2,1,0:T(8,128)(2,1)} %copy.65), calls=%async_computation.5 | async-start | bytes 4194304 | tf_op jit(solution)/shard_map/all_to_all | solution.py:159
  356.1 1.6 copy-start.1
  356.1 1.7 copy-start.4
  356.2 1.8 copy-start.5
  358.0 2.2 copy-start.7
  358.0 2.2 copy-start.8
  358.0 2.2 copy-start.9
Sparse Core Ops, SparseCore 0:
  10.8 103.1 all-gather.4
  121.7 147.7 all-gather.2
Sparse Core Ops, SparseCore 1:
  118.2 174.3 all-reduce.2
  297.1 236.3 reduce-scatter.1
where the time goes:
time: 546 us; the launch traced here: 543 us
  waiting for transfers between devices  414 us (76%)
  matrix products  45.7 us (8%)
  starting transfers between devices  39.6 us (7%)
  local copies, waits for them, and re-layouts  24.2 us (4%)
  between operations  15.6 us (3%)
    psum x1, waiting for transfers between devices, per_device(): lax.psum(apply_down(arrived_input, down_portion, arrived_adapter_index, i...  163 us
    reduce_scatter x1, waiting for transfers between devices, per_device(): lax.psum_scatter(input_terms.astype(jnp.bfloat16), 'tensor', scatter_dime...  131 us
    all_to_all x1, waiting for transfers between devices, per_device(): lax.all_to_all(send_x, 'adapter', split_axis=0, concat_axis=0, tiled=True)  40.4 us
    all_to_all x1, waiting for transfers between devices, per_device(): lax.all_to_all(send_dy, 'adapter', split_axis=0, concat_axis=0, tiled=True)  35.9 us
    all_to_all x1, waiting for transfers between devices, per_device(): lax.all_to_all(adapter_gradient, 'adapter', split_axis=0, concat_axis=0,...  20.8 us
    all_to_all x1, waiting for transfers between devices, per_device(): lax.all_to_all(adapter_output, 'adapter', split_axis=0, concat_axis=0, ti...  20.7 us
    all_to_all x1, starting transfers between devices, per_device(): lax.all_to_all(adapter_output, 'adapter', split_axis=0, concat_axis=0, ti...  14.8 us
    dot_general x1, matrix products, per_device(): jnp.dot(lax.all_gather(tokens, 'tensor', axis=1, tiled=True), weight_cols...  11.1 us
  transfers between devices with their start and end apart: 9, of which 7 were waited for; matrix products, arithmetic and copies ran while one was open for 13% of the time, Pallas kernels for 0%

commit v1 on v0

v1 whole, which is shorter than its diff:
```python
import functools

import jax
import jax.numpy as jnp
from jax import lax
from jax.experimental import pallas as pl
from jax.experimental.pallas import tpu as pltpu
from jax.sharding import Mesh
from jax.sharding import PartitionSpec as P

ADAM_STEP = 10

adapter_scale = 0.5
beta_one = 0.9
beta_two = 0.999
adam_eps = 1e-08
weight_decay = 0.01
learn_rate = 0.001

VMEM = pl.BlockSpec(memory_space=pltpu.VMEM)
SMEM = pl.BlockSpec(memory_space=pltpu.SMEM)
ADAPTER = ("xl", "y", "c")
TENSOR = ("xh", "z")
NT = (((1,), (1,)), ((), ()))
TN = (((0,), (0,)), ((), ()))
NN = (((1,), (0,)), ((), ()))


def dot(a, b, dims):
    return lax.dot_general(a, b, dims, preferred_element_type=jnp.float32)


def call(kernel, out_shape, args, scalars, flops, moved, limit=40, scratch=()):
    return pl.pallas_call(
        kernel,
        out_shape=out_shape,
        in_specs=[SMEM] * len(scalars) + [VMEM] * len(args),
        out_specs=jax.tree.map(lambda _: VMEM, out_shape),
        scratch_shapes=list(scratch),
        compiler_params=pltpu.CompilerParams(vmem_limit_bytes=limit * 2**20),
        cost_estimate=pl.CostEstimate(flops=flops, bytes_accessed=moved, transcendentals=0),
    )(*scalars, *args)


def decoupled_adam(parameter, moment, second, gradient):
    moment_new = beta_one * moment + (1.0 - beta_one) * gradient
    second_new = beta_two * second + (1.0 - beta_two) * gradient * gradient
    bias_first = 1.0 - beta_one**ADAM_STEP
    bias_second = 1.0 - beta_two**ADAM_STEP
    update = (
        moment_new / bias_first / (jnp.sqrt(second_new / bias_second) + adam_eps)
        + weight_decay * parameter
    )
    return (parameter - learn_rate * update, moment_new, second_new)


def select_kernel(slot_ref, down_ref, up_ref, send_ref, both_ref):
    rank = down_ref.shape[1]
    both_ref[:, :rank] = down_ref[...].astype(jnp.bfloat16)
    both_ref[:, rank:] = up_ref[...].astype(jnp.bfloat16)
    held = down_ref.shape[0]

    @pl.loop(0, send_ref.shape[0])
    def _(peer):
        send_ref[peer] = both_ref[jnp.minimum(slot_ref[peer], held - 1)]


def low_kernel(owner_ref, x_ref, dy_ref, weight_ref, low_ref):
    tiles = owner_ref.shape[0]
    height = x_ref.shape[0] // tiles
    rank = weight_ref.shape[1] // 2
    for j in range(tiles):
        rows = pl.ds(j * height, height)
        weight = weight_ref[owner_ref[j]]
        fwd = dot(x_ref[rows], weight, NT)
        bwd = dot(dy_ref[rows], weight, NT)
        lane = lax.broadcasted_iota(jnp.int32, fwd.shape, 1)
        low_ref[rows] = jnp.where(lane < rank, fwd, bwd).astype(jnp.bfloat16)


def grad_kernel(owner_ref, low_ref, x_ref, dy_ref, weight_ref, send_ref, out_ref, back_ref):
    tiles = owner_ref.shape[0]
    height = x_ref.shape[0] // tiles
    rank = weight_ref.shape[1] // 2
    send_ref[...] = jnp.zeros_like(send_ref)
    for j in range(tiles):
        rows = pl.ds(j * height, height)
        owner = owner_ref[j]
        weight = weight_ref[owner]
        low = low_ref[rows]
        fwd, bwd = low[:, :rank], low[:, rank:]
        out_ref[rows] = (adapter_scale * dot(fwd, weight[rank:], NN)).astype(jnp.bfloat16)
        back_ref[rows] = (adapter_scale * dot(bwd, weight[:rank], NN)).astype(jnp.bfloat16)
        up_part = dot(low, dy_ref[rows], TN)[:rank]
        down_part = dot(low, x_ref[rows], TN)[rank:]
        part = jnp.concatenate([down_part, up_part], axis=0)
        send_ref[owner] = (adapter_scale * part).astype(jnp.bfloat16)


def adam_kernel(slot_ref, part_ref, pd, pu, md, vd, mu, vu, npd, npu, nmd, nvd, nmu, nvu, acc):
    held, rank, _ = pd.shape
    acc[...] = jnp.zeros_like(acc)

    @pl.loop(0, part_ref.shape[0])
    def _(peer):
        slot = slot_ref[peer]

        @pl.when(slot < held)
        def _():
            acc[slot] += part_ref[peer].astype(jnp.float32)

    for k in range(held):
        npd[k], nmd[k], nvd[k] = decoupled_adam(pd[k], md[k], vd[k], acc[k, :rank])
        npu[k], nmu[k], nvu[k] = decoupled_adam(pu[k], mu[k], vu[k], acc[k, rank:])


def back_kernel(at_ref, mine_ref, theirs_ref, *refs):
    weights, out_ref = refs[:-1], refs[-1]
    xh = at_ref[0]
    for i, weight in enumerate(weights):
        total = dot(mine_ref[...], weight[xh], NT) + dot(theirs_ref[...], weight[1 - xh], NT)
        out_ref[at_ref[1 + i]] = total.astype(jnp.bfloat16)


def forward_kernel(at_ref, x_ref, *refs, theirs):
    weights, out_ref = refs[:-1], refs[-1]
    column = 1 - at_ref[0] if theirs else at_ref[0]
    total = dot(x_ref[at_ref[1]], weights[0][column], NN)
    for i, weight in enumerate(weights[1:], 1):
        total += dot(x_ref[at_ref[1 + i]], weight[column], NN)
    out_ref[...] = total.astype(out_ref.dtype)


def per_device(
    tokens,
    cotangent,
    frozen_weight,
    adapter_per_tile,
    tile_token_length,
    adapter_down_weight,
    adapter_up_weight,
    down_first_moment,
    down_second_moment,
    up_first_moment,
    up_second_moment,
):
    bf16, f32 = jnp.bfloat16, jnp.float32
    tok_rows, width = tokens.shape
    tile_count = adapter_per_tile.shape[1]
    tile_rows = tok_rows // tile_count
    held, rank, _ = adapter_down_weight.shape
    owners = lax.axis_size(ADAPTER)
    peers = lax.axis_size(TENSOR)
    planes = lax.axis_size("z")
    ys = lax.axis_size("y")
    xl, y, c, xh = (lax.axis_index(n) for n in ("xl", "y", "c", "xh"))

    adapters_here = adapter_per_tile[0]
    owner_of = adapters_here // held
    chosen = owner_of[None, :] == jnp.arange(owners, dtype=jnp.int32)[:, None]
    asked = jnp.sum(jnp.where(chosen, adapters_here[None, :] % held - held, 0), axis=1) + held
    slots = lax.all_to_all(
        asked.reshape(owners, 1, 1), ADAPTER, split_axis=0, concat_axis=0, tiled=True
    ).reshape(owners)

    swap = [(0, 1), (1, 0)]
    position = jnp.arange(tile_rows, dtype=jnp.int32)
    kept = position[None, :] < tile_token_length[0][:, None]
    dy = jnp.where(
        kept[:, :, None],
        cotangent.reshape(tile_count, tile_rows, width),
        jnp.zeros((), bf16),
    ).reshape(tok_rows, width)
    dy_theirs = lax.ppermute(dy, "xh", swap)

    x_all = lax.all_gather(tokens, "z", axis=0)

    sites = [(0, 0), (1, 0), (0, 1), (1, 1)]
    place = [a * 2 + b for a, b in sites]
    first = lax.ppermute(
        frozen_weight, ("xl", "xh"), [(place[0], place[1]), (place[1], place[2]), (place[2], place[0])]
    )
    second = lax.ppermute(
        frozen_weight, ("xl", "xh"), [(place[1], place[3]), (place[2], place[1]), (place[3], place[2])]
    )
    x_site = xh * 2 + xl
    block_a = jnp.where(x_site == 0, frozen_weight, jnp.where(x_site == 3, second, first))
    block_b = jnp.where(x_site == 3, frozen_weight, jnp.where(x_site == 0, first, second))
    here = jnp.stack([block_a, block_b])

    sent = call(
        select_kernel,
        jax.ShapeDtypeStruct((owners, 2 * rank, width), bf16),
        [adapter_down_weight, adapter_up_weight],
        [slots],
        0,
        3 * 2**20,
        scratch=[pltpu.VMEM((held, 2 * rank, width), bf16)],
    )
    here, sent, dy_theirs = lax.optimization_barrier((here, sent, dy_theirs))
    tile_weights = lax.all_to_all(sent, ADAPTER, split_axis=0, concat_axis=0, tiled=True)

    up_ring = [(i, (i + 1) % ys) for i in range(ys)]
    down_ring = [(i, (i - 1) % ys) for i in range(ys)]
    below = lax.ppermute(here, "y", up_ring)
    above = lax.ppermute(here, "y", down_ring)
    far = jnp.stack(
        [lax.ppermute(below[0], "y", up_ring), lax.ppermute(above[1], "y", down_ring)]
    )

    tile_weights, _, _ = lax.optimization_barrier((tile_weights, below, above))
    low_part = call(
        low_kernel,
        jax.ShapeDtypeStruct((tok_rows, 2 * rank), bf16),
        [tokens, dy, tile_weights],
        [owner_of],
        8 * tok_rows * width * rank,
        3 * 2**20,
    )
    share = tok_rows // peers
    low_terms = lax.all_to_all(
        low_part.reshape(peers, share, 2 * rank), TENSOR, split_axis=0, concat_axis=0, tiled=True
    )
    far, low_terms = lax.optimization_barrier((far, low_terms))
    mine = [here, below, above, far]
    weights = mine + [lax.ppermute(w, "c", swap) for w in mine]
    steps = [0, ys - 1, 1, 2]
    at = jnp.stack(
        [xh]
        + [2 * ((y + s) % ys) + c for s in steps]
        + [2 * ((y + s) % ys) + 1 - c for s in steps]
    ).astype(jnp.int32)

    big = 2 * tok_rows * planes * width * width
    parts = call(
        back_kernel,
        jax.ShapeDtypeStruct((planes, tok_rows, width), bf16),
        [dy, dy_theirs, *weights],
        [at],
        2 * big,
        13 * 2**20,
    )
    parts, low_terms = lax.optimization_barrier((parts, low_terms))
    input_sum = lax.psum_scatter(parts, "z", scatter_dimension=0)

    low_share = jnp.sum(low_terms.astype(f32), axis=0).astype(bf16)
    low = lax.all_to_all(
        jnp.broadcast_to(low_share[None], (peers, share, 2 * rank)),
        TENSOR,
        split_axis=0,
        concat_axis=0,
        tiled=True,
    ).reshape(tok_rows, 2 * rank)
    grads_sent, lora_out, lora_grad = call(
        grad_kernel,
        (
            jax.ShapeDtypeStruct((owners, 2 * rank, width), bf16),
            jax.ShapeDtypeStruct((tok_rows, width), bf16),
            jax.ShapeDtypeStruct((tok_rows, width), bf16),
        ),
        [low, tokens, dy, tile_weights],
        [owner_of],
        16 * tok_rows * width * rank,
        6 * 2**20,
    )
    grad_parts = lax.all_to_all(grads_sent, ADAPTER, split_axis=0, concat_axis=0, tiled=True)

    x_all, grads_sent_done = lax.optimization_barrier((x_all, lora_out))
    lora_out = grads_sent_done

    out_theirs = call(
        functools.partial(forward_kernel, theirs=True),
        jax.ShapeDtypeStruct((tok_rows, width), bf16),
        [x_all, *weights],
        [at],
        big,
        8 * 2**20,
    )
    out_swapped = lax.ppermute(out_theirs, "xh", swap)
    out_mine = call(
        functools.partial(forward_kernel, theirs=False),
        jax.ShapeDtypeStruct((tok_rows, width), f32),
        [x_all, *weights],
        [at],
        big,
        8 * 2**20,
    )

    lanes = 128
    state = (
        adapter_down_weight,
        adapter_up_weight,
        down_first_moment,
        down_second_moment,
        up_first_moment,
        up_second_moment,
    )
    state_spec = pl.BlockSpec((held, rank, lanes), lambda i: (0, 0, i))
    fresh = pl.pallas_call(
        adam_kernel,
        grid=(width // lanes,),
        out_shape=[jax.ShapeDtypeStruct(adapter_down_weight.shape, f32)] * 6,
        in_specs=[SMEM, pl.BlockSpec((owners, 2 * rank, lanes), lambda i: (0, 0, i))]
        + [state_spec] * 6,
        out_specs=[state_spec] * 6,
        scratch_shapes=[pltpu.VMEM((held, 2 * rank, lanes), f32)],
        compiler_params=pltpu.CompilerParams(vmem_limit_bytes=60 * 2**20),
        cost_estimate=pl.CostEstimate(
            flops=60 * held * rank * width, bytes_accessed=8 * 2**20, transcendentals=0
        ),
    )(slots, grad_parts, *state)

    output = (out_mine + out_swapped.astype(f32) + lora_out.astype(f32)).astype(bf16)
    token_gradient = (input_sum.astype(f32) + lora_grad.astype(f32)).astype(bf16)
    return (output, token_gradient, *fresh)


def solution(mesh):
    split = Mesh(mesh.devices.reshape(2, 4, 2, 2, 8), ("xl", "y", "c", "xh", "z"))
    matrix = P(ADAPTER, TENSOR)
    table = P(ADAPTER, None)
    state = P(ADAPTER, None, TENSOR)
    return jax.shard_map(
        per_device,
        mesh=split,
        in_specs=(matrix,) * 3 + (table,) * 2 + (state,) * 6,
        out_specs=(matrix,) * 2 + (state,) * 6,
        check_vma=False,
    )
```

time: 546 us -> 227 us (0.42)
  waiting for transfers between devices: 414 us -> 84.1 us
  matrix products: 45.7 us -> 0 us
  Pallas kernels: 0 us -> 27.3 us
  blocking collectives: 0 us -> 12.6 us
  other arithmetic: 3.65 us -> 12.5 us
  starting transfers between devices: 39.6 us -> 46.3 us
    psum x1 -> x0, waiting for transfers between devices: 163 us -> none  [per_device(): lax.psum(apply_down(arrived_input, down_portion, arrived_adapter_index, i...]
    reduce_scatter x1, waiting for transfers between devices: 131 us -> 0.01 us  [per_device(): input_sum = lax.psum_scatter(parts, 'z', scatter_dimension=0)]
    all_to_all x5 -> x4, waiting for transfers between devices: 119 us -> 35 us  [the longest x1 16 us: per_device(): lax.all_to_all(grads_sent, ADAPTER, split_axis=0, concat_axis=0, tiled=True)]
    ppermute x0 -> x12, waiting for transfers between devices: none -> 48.4 us  [the longest x1 45.9 us: per_device(): below = lax.ppermute(here, 'y', up_ring)]
    dot_general x12 -> x0, matrix products: 45.7 us -> none  [the longest x1 11.1 us: per_device(): jnp.dot(lax.all_gather(tokens, 'tensor', axis=1, tiled=True), weight_cols...]
    pallas_call x0 -> x7, Pallas kernels: none -> 27.3 us  [the longest x6 21.8 us: call(): pl.pallas_call(kernel, out_shape=out_shape, in_specs=[SMEM] * len(scalars...]
    unnamed x24 -> x52, local copies, waits for them, and re-layouts: 1.87 us -> 24.6 us
    ppermute x0 -> x12, starting transfers between devices: none -> 19 us  [the longest x1 6.25 us: per_device(): lax.ppermute(frozen_weight, ('xl', 'xh'), [(place[0], place[1]), (place[1...]
  transfers between devices with their start and end apart: 9 -> 18, of which waited for: 7 -> 5; matrix products, arithmetic and copies ran while one was open for 13% -> 6% of each run, Pallas kernels for 0% -> 12%
where the time goes in v1:
time: 227 us; the launch traced here: 224 us
  waiting for transfers between devices  84.1 us (37%)
  starting transfers between devices  46.3 us (20%)
  Pallas kernels  27.3 us (12%)
  local copies, waits for them, and re-layouts  27.2 us (12%)
  between operations  14.3 us (6%)
  blocking collectives  12.6 us (6%)
  other arithmetic  12.5 us (6%)
    ppermute x1, waiting for transfers between devices, per_device(): below = lax.ppermute(here, 'y', up_ring)  45.9 us
    unnamed x52, local copies, waits for them, and re-layouts  24.6 us
    pallas_call x6, Pallas kernels, call(): pl.pallas_call(kernel, out_shape=out_shape, in_specs=[SMEM] * len(scalars...  21.8 us
    all_to_all x1, waiting for transfers between devices, per_device(): lax.all_to_all(grads_sent, ADAPTER, split_axis=0, concat_axis=0, tiled=True)  16 us
    all_to_all x1, waiting for transfers between devices, per_device(): lax.all_to_all(asked.reshape(owners, 1, 1), ADAPTER, split_axis=0, concat...  14.5 us
    all_to_all x1, blocking collectives, per_device(): lax.all_to_all(jnp.broadcast_to(low_share[None], (peers, share, 2 * rank)...  12.6 us
    all_to_all x1, starting transfers between devices, per_device(): lax.all_to_all(low_part.reshape(peers, share, 2 * rank), TENSOR, split_ax...  8.29 us
    all_to_all x1, starting transfers between devices, per_device(): lax.all_to_all(grads_sent, ADAPTER, split_axis=0, concat_axis=0, tiled=True)  6.89 us
  transfers between devices with their start and end apart: 18, of which 5 were waited for; matrix products, arithmetic and copies ran while one was open for 6% of the time, Pallas kernels for 12%

profile of v1, /device:TPU:1, one launch (start us, length us, event | category | flops | bytes accessed | tf_op | source)
XLA Modules:
  0.0 224.5 jit_solution(3484319933305559427)
XLA Ops:
  9.4 6.3 %collective-permute-start.1 = (bf16[512,512]{1,0:T(8,128)(2,1)}, bf16[512,512]{1,0:T(8,128)(2,1)}, u32[]{:S(2)}, u32[]{:S(2)}) collective-permute-start(bf16[512,512]{1,0:T(8,128)(2,1)} %param.13), channel_id=1, source_target_pairs={{0,128},{128,8},{8,0},{1,129},{129,9},{9,1},{2,130},{130,10},{10,2... | collective-permute-start | bytes 1572872 | tf_op jit(solution)/shard_map/ppermute | solution.py:180
  19.8 5.7 %all-to-all-start = ((s32[16,1,1]{2,1,0:T(1,128)}), s32[16,1,1]{2,1,0:T(1,128)S(1)}, u32[]{:S(2)}, u32[]{:S(2)}) async-start(s32[16,1,1]{2,1,0:T(1,128)} %copy.21), calls=%async_computation | async-start | bytes 16384 | tf_op jit(solution)/shard_map/all_to_all | solution.py:162
  25.5 14.5 %all-to-all-done = s32[16,1,1]{2,1,0:T(1,128)S(1)} async-done(((s32[16,1,1]{2,1,0:T(1,128)}), s32[16,1,1]{2,1,0:T(1,128)S(1)}, u32[]{:S(2)}, u32[]{:S(2)}) %all-to-all-start) | async-done | bytes 96 | tf_op jit(solution)/shard_map/all_to_all | solution.py:162
  43.3 2.2 select_bitcast_fusion.1
  45.7 6.4 %all-to-all-start.1 = ((bf16[16,128,512]{2,1,0:T(8,128)(2,1)}), bf16[16,128,512]{2,1,0:T(8,128)(2,1)S(1)}, u32[]{:S(2)}, u32[]{:S(2)}) async-start(bf16[16,128,512]{2,1,0:T(8,128)(2,1)} %copy-done.5), calls=%async_computation.1 | async-start | bytes 4194304 | tf_op jit(solution)/shard_map/all_to_all | solution.py:201
  54.8 45.9 %collective-permute-done.3.refs_1_ = bf16[2,512,512]{2,1,0:T(8,128)(2,1)S(1)} collective-permute-done((bf16[2,512,512]{2,1,0:T(8,128)(2,1)S(1)}, bf16[2,512,512]{2,1,0:T(8,128)(2,1)S(1)}, u32[]{:S(2)}, u32[]{:S(2)}) %collective-permute-start.3) | collective-permute-done | bytes 1048608 | tf_op jit(solution)/shard_map/ppermute | solution.py:205
  102.5 2.7 %collective-permute-start.6 = (bf16[512,512]{1,0:T(8,128)(2,1)}, bf16[512,512]{1,0:T(8,128)(2,1)}, u32[]{:S(2)}, u32[]{:S(2)}) collective-permute-start(bf16[512,512]{1,0:T(8,128)(2,1)} %slice_bitcast_fusion), channel_id=1, source_target_pairs={{0,96},{32,0},{64,32},{96,64},{1,97},{33,1},{65,33},{97,65},{2,98}... | collective-permute-start | bytes 1572872 | tf_op jit(solution)/shard_map/ppermute | solution.py:208
  106.2 2.1 shard_map.171
  108.4 8.3 %all-to-all-start.2 = ((bf16[16,32,128]{2,1,0:T(8,128)(2,1)}), bf16[16,32,128]{2,1,0:T(8,128)(2,1)S(1)}, u32[]{:S(2)}, u32[]{:S(2)}) async-start(bf16[16,32,128]{2,1,0:T(8,128)(2,1)} %bitcast.22), calls=%async_computation.2 | async-start | bytes 262144 | tf_op jit(solution)/shard_map/all_to_all | solution.py:221
  118.9 2.3 %pad_maximum_fusion.1.refs_3_ = bf16[2,512,512]{2,1,0:T(8,128)(2,1)} fusion(bf16[1,512,512]{2,1,0:T(8,128)(2,1)} %bitcast.21, bf16[1,512,512]{2,1,0:T(8,128)(2,1)} %bitcast.19), kind=kLoop, calls=%fused_computation.1 | loop fusion | flops 524288 | bytes 2097152 | tf_op jit(solution)/shard_map/stack | solution.py:207
  121.2 4.4 %all-to-all-done.2 = bf16[16,32,128]{2,1,0:T(8,128)(2,1)S(1)} async-done(((bf16[16,32,128]{2,1,0:T(8,128)(2,1)}), bf16[16,32,128]{2,1,0:T(8,128)(2,1)S(1)}, u32[]{:S(2)}, u32[]{:S(2)}) %all-to-all-start.2) | async-done | bytes 131104 | tf_op jit(solution)/shard_map/all_to_all | solution.py:221
  125.6 2.7 %collective-permute-start.10 = (bf16[2,512,512]{2,1,0:T(8,128)(2,1)}, bf16[2,512,512]{2,1,0:T(8,128)(2,1)}, u32[]{:S(2)}, u32[]{:S(2)}) collective-permute-start(bf16[2,512,512]{2,1,0:T(8,128)(2,1)} %pad_maximum_fusion.1.refs_3_), channel_id=1, source_target_pairs={{0,16},{16,0},{1,17},{17,1},{2,18},{18,2},{3,19},{19,3},{4,20},{20... | collective-permute-start | bytes 3145736 | tf_op jit(solution)/shard_map/ppermute | solution.py:226
  128.4 2.5 %collective-permute-done.10.refs_7_ = bf16[2,512,512]{2,1,0:T(8,128)(2,1)} collective-permute-done((bf16[2,512,512]{2,1,0:T(8,128)(2,1)}, bf16[2,512,512]{2,1,0:T(8,128)(2,1)}, u32[]{:S(2)}, u32[]{:S(2)}) %collective-permute-start.10) | collective-permute-done | bytes 1048608 | tf_op jit(solution)/shard_map/ppermute | solution.py:226
  134.6 7.0 %shard_map.172 = bf16[8,512,512]{2,1,0:T(8,128)(2,1)S(1)} custom-call(s32[9]{0:T(128)S(1)} %stack.57.at_ref, bf16[512,512]{1,0:T(8,128)(2,1)} %broadcast_select_fusion.dy_ref.mine_ref, bf16[512,512]{1,0:T(8,128)(2,1)} %collective-permute-done.2.theirs_ref, bf16[2,512,512]{2,1,0:T(8,128)(2,1)S(1)} %pad_maximum_fusion.refs_0_, ...), custom_call_target="tpu_custom_call" | custom-call | flops 4294967296 | bytes 13631488 | tf_op jit(solution)/shard_map/pallas_call | solution.py:34
  141.7 2.0 copy-done.16
  143.8 12.6 %all_to_all.25 = bf16[16,32,128]{2,1,0:T(8,128)(2,1)S(1)} all-to-all(bf16[16,32,128]{2,1,0:T(8,128)(2,1)S(1)} %broadcast_in_dim.41), channel_id=1, replica_groups=mesh['xl'=2,'y'=4,'c'=2,'xh'=2,'z'=8] {'xh','z'}, dimensions={0} | all-to-all | bytes 262144 | tf_op jit(solution)/shard_map/all_to_all | solution.py:247
  162.3 6.9 %all-to-all-start.4 = ((bf16[16,128,512]{2,1,0:T(8,128)(2,1)}), bf16[16,128,512]{2,1,0:T(8,128)(2,1)}, u32[]{:S(2)}, u32[]{:S(2)}) async-start(bf16[16,128,512]{2,1,0:T(8,128)(2,1)} %copy-done.17), calls=%async_computation.5 | async-start | bytes 4194304 | tf_op jit(solution)/shard_map/all_to_all | solution.py:266
  169.3 2.2 copy-done
  175.2 5.4 %shard_map.175 = bf16[512,512]{1,0:T(8,128)(2,1)} custom-call(s32[9]{0:T(128)S(1)} %stack.57.at_ref, bf16[8,512,512]{2,1,0:T(8,128)(2,1)S(1)} %bitcast.42, bf16[2,512,512]{2,1,0:T(8,128)(2,1)S(1)} %pad_maximum_fusion.refs_0_, bf16[2,512,512]{2,1,0:T(8,128)(2,1)S(1)} %copy-done.8, bf16[2,512,512]{2,1,0:T(8,128)(2,1)S(1)} %copy-done.12, ...), custom_call_target="tpu_custom_call" | custom-call | flops 2147483648 | bytes 8388608 | tf_op jit(solution)/shard_map/pallas_call | solution.py:34
  181.4 16.0 %all-to-all-done.4.part_ref = bf16[16,128,512]{2,1,0:T(8,128)(2,1)} async-done(((bf16[16,128,512]{2,1,0:T(8,128)(2,1)}), bf16[16,128,512]{2,1,0:T(8,128)(2,1)}, u32[]{:S(2)}, u32[]{:S(2)}) %all-to-all-start.4) | async-done | bytes 2097184 | tf_op jit(solution)/shard_map/all_to_all | solution.py:266
  197.5 5.6 %shard_map.176 = (f32[4,64,512]{2,1,0:T(8,128)}, f32[4,64,512]{2,1,0:T(8,128)}, f32[4,64,512]{2,1,0:T(8,128)}, f32[4,64,512]{2,1,0:T(8,128)}, f32[4,64,512]{2,1,0:T(8,128)}, /*index=5*/f32[4,64,512]{2,1,0:T(8,128)}) custom-call(s32[16]{0:T(128)} %copy-done.24, bf16[16,128,512]{2,1,0:T(8,128)(2,1)} %all-to-all-done.4.part_ref, f32[4,64,512]{2,1,0:T(8,128)} %pd.1, ...), custom_call_target="tpu_custom_call" | custom-call | flops 7864320 | bytes 8388608 | tf_op jit(solution)/shard_map/pallas_call | solution.py:299
  203.1 2.2 copy-done.1
  208.9 4.6 %shard_map.174 = f32[512,512]{1,0:T(8,128)S(1)} custom-call(s32[9]{0:T(128)S(1)} %stack.57.at_ref, bf16[8,512,512]{2,1,0:T(8,128)(2,1)S(1)} %bitcast.43, bf16[2,512,512]{2,1,0:T(8,128)(2,1)S(1)} %pad_maximum_fusion.refs_0_, bf16[2,512,512]{2,1,0:T(8,128)(2,1)S(1)} %copy-done.9, bf16[2,512,512]{2,1,0:T(8,128)(2,1)S(1)} %copy-done.13, ...), custom_call_target="tpu_custom_call" | custom-call | flops 2147483648 | bytes 8388608 | tf_op jit(solution)/shard_map/pallas_call | solution.py:34
  213.5 2.1 add_convert_fusion
  (92 shorter events, 37.5 us)
Async XLA Ops:
  7.2 162.1 %all-gather.3.cloned.1.call-start = ((), (), s32[]{:S(2)}) async-start(), calls=%async_computation.7 | async-start | bytes 4718592 | tf_op jit(solution)/shard_map/all_gather | solution.py:176
  7.9 35.4 %collective-permute-start = (bf16[512,512]{1,0:T(8,128)(2,1)}, bf16[512,512]{1,0:T(8,128)(2,1)}, u32[]{:S(2)}, u32[]{:S(2)}) collective-permute-start(bf16[512,512]{1,0:T(8,128)(2,1)} %param.13), channel_id=1, source_target_pairs={{128,136},{8,128},{136,8},{129,137},{9,129},{137,9},{130,138},{10,... | collective-permute-start | bytes 1572872 | tf_op jit(solution)/shard_map/ppermute | solution.py:183
  9.4 34.0 %collective-permute-start.1 = (bf16[512,512]{1,0:T(8,128)(2,1)}, bf16[512,512]{1,0:T(8,128)(2,1)}, u32[]{:S(2)}, u32[]{:S(2)}) collective-permute-start(bf16[512,512]{1,0:T(8,128)(2,1)} %param.13), channel_id=1, source_target_pairs={{0,128},{128,8},{8,0},{1,129},{129,9},{9,1},{2,130},{130,10},{10,2... | collective-permute-start | bytes 1572872 | tf_op jit(solution)/shard_map/ppermute | solution.py:180
  18.3 27.3 %collective-permute-start.2 = (bf16[512,512]{1,0:T(8,128)(2,1)}, bf16[512,512]{1,0:T(8,128)(2,1)}, u32[]{:S(2)}, u32[]{:S(2)}) collective-permute-start(bf16[512,512]{1,0:T(8,128)(2,1)} %broadcast_select_fusion.dy_ref.mine_ref), channel_id=1, source_target_pairs={{0,8},{8,0},{1,9},{9,1},{2,10},{10,2},{3,11},{11,3},{4,12},{12,4},... | collective-permute-start | bytes 1572872 | tf_op jit(solution)/shard_map/ppermute | solution.py:174
  19.8 20.2 %all-to-all-start = ((s32[16,1,1]{2,1,0:T(1,128)}), s32[16,1,1]{2,1,0:T(1,128)S(1)}, u32[]{:S(2)}, u32[]{:S(2)}) async-start(s32[16,1,1]{2,1,0:T(1,128)} %copy.21), calls=%async_computation | async-start | bytes 16384 | tf_op jit(solution)/shard_map/all_to_all | solution.py:162
  42.5 3.1 %copy-start.24 = (s32[16]{0:T(128)}, s32[16]{0:T(128)S(1)}, u32[]{:S(2)}) copy-start(s32[16]{0:T(128)S(1)} %reduce.1.slot_ref) | copy-start | bytes 196
  43.3 2.3 %copy-start.5 = (bf16[16,128,512]{2,1,0:T(8,128)(2,1)}, bf16[16,128,512]{2,1,0:T(8,128)(2,1)S(1)}, u32[]{:S(2)}) copy-start(bf16[16,128,512]{2,1,0:T(8,128)(2,1)S(1)} %shard_map.170) | copy-start | bytes 6291460
  45.7 59.5 %all-to-all-start.1 = ((bf16[16,128,512]{2,1,0:T(8,128)(2,1)}), bf16[16,128,512]{2,1,0:T(8,128)(2,1)S(1)}, u32[]{:S(2)}, u32[]{:S(2)}) async-start(bf16[16,128,512]{2,1,0:T(8,128)(2,1)} %copy-done.5), calls=%async_computation.1 | async-start | bytes 4194304 | tf_op jit(solution)/shard_map/all_to_all | solution.py:201
  52.1 53.1 %copy-start.25 = (s32[1,4]{1,0:T(1,128)S(1)}, s32[1,4]{1,0:T(1,128)}, u32[]{:S(2)}) copy-start(s32[1,4]{1,0:T(1,128)} %param.14) | copy-start | bytes 52
  52.1 48.6 %collective-permute-start.3 = (bf16[2,512,512]{2,1,0:T(8,128)(2,1)S(1)}, bf16[2,512,512]{2,1,0:T(8,128)(2,1)S(1)}, u32[]{:S(2)}, u32[]{:S(2)}) collective-permute-start(bf16[2,512,512]{2,1,0:T(8,128)(2,1)S(1)} %pad_maximum_fusion.refs_0_), channel_id=1, source_target_pairs={{0,32},{32,64},{64,96},{96,0},{1,33},{33,65},{65,97},{97,1},{2,34}... | collective-permute-start | bytes 3145736 | tf_op jit(solution)/shard_map/ppermute | solution.py:205
  53.5 48.1 %collective-permute-start.4 = (bf16[2,512,512]{2,1,0:T(8,128)(2,1)S(1)}, bf16[2,512,512]{2,1,0:T(8,128)(2,1)S(1)}, u32[]{:S(2)}, u32[]{:S(2)}) collective-permute-start(bf16[2,512,512]{2,1,0:T(8,128)(2,1)S(1)} %pad_maximum_fusion.refs_0_), channel_id=1, source_target_pairs={{0,96},{32,0},{64,32},{96,64},{1,97},{33,1},{65,33},{97,65},{2,98}... | collective-permute-start | bytes 3145736 | tf_op jit(solution)/shard_map/ppermute | solution.py:206
  100.7 4.5 %copy-start.6 = (bf16[2,512,512]{2,1,0:T(8,128)(2,1)}, bf16[2,512,512]{2,1,0:T(8,128)(2,1)S(1)}, u32[]{:S(2)}) copy-start(bf16[2,512,512]{2,1,0:T(8,128)(2,1)S(1)} %collective-permute-done.3.refs_1_) | copy-start | bytes 3145732
  101.6 17.3 %collective-permute-start.5 = (bf16[512,512]{1,0:T(8,128)(2,1)}, bf16[512,512]{1,0:T(8,128)(2,1)}, u32[]{:S(2)}, u32[]{:S(2)}) collective-permute-start(bf16[512,512]{1,0:T(8,128)(2,1)} %slice_bitcast_fusion.1), channel_id=1, source_target_pairs={{0,32},{32,64},{64,96},{96,0},{1,33},{33,65},{65,97},{97,1},{2,34}... | collective-permute-start | bytes 1572872 | tf_op jit(solution)/shard_map/ppermute | solution.py:208
  101.6 3.6 %copy-start.10 = (bf16[2,512,512]{2,1,0:T(8,128)(2,1)}, bf16[2,512,512]{2,1,0:T(8,128)(2,1)S(1)}, u32[]{:S(2)}) copy-start(bf16[2,512,512]{2,1,0:T(8,128)(2,1)S(1)} %collective-permute-done.4.refs_2_) | copy-start | bytes 3145732
  102.5 16.4 %collective-permute-start.6 = (bf16[512,512]{1,0:T(8,128)(2,1)}, bf16[512,512]{1,0:T(8,128)(2,1)}, u32[]{:S(2)}, u32[]{:S(2)}) collective-permute-start(bf16[512,512]{1,0:T(8,128)(2,1)} %slice_bitcast_fusion), channel_id=1, source_target_pairs={{0,96},{32,0},{64,32},{96,64},{1,97},{33,1},{65,33},{97,65},{2,98}... | collective-permute-start | bytes 1572872 | tf_op jit(solution)/shard_map/ppermute | solution.py:208
  108.4 17.2 %all-to-all-start.2 = ((bf16[16,32,128]{2,1,0:T(8,128)(2,1)}), bf16[16,32,128]{2,1,0:T(8,128)(2,1)S(1)}, u32[]{:S(2)}, u32[]{:S(2)}) async-start(bf16[16,32,128]{2,1,0:T(8,128)(2,1)} %bitcast.22), calls=%async_computation.2 | async-start | bytes 262144 | tf_op jit(solution)/shard_map/all_to_all | solution.py:221
  116.7 99.0 %reduce-scatter.2.cloned.1.call-start = ((), (), s32[]{:S(2)}) async-start(), calls=%async_computation.6 | async-start | bytes 4718592 | tf_op jit(solution)/shard_map/reduce_scatter | solution.py:244
  116.7 11.7 %collective-permute-start.7 = (bf16[2,512,512]{2,1,0:T(8,128)(2,1)S(1)}, bf16[2,512,512]{2,1,0:T(8,128)(2,1)}, u32[]{:S(2)}, u32[]{:S(2)}) collective-permute-start(bf16[2,512,512]{2,1,0:T(8,128)(2,1)S(1)} %pad_maximum_fusion.refs_0_), channel_id=1, source_target_pairs={{0,16},{16,0},{1,17},{17,1},{2,18},{18,2},{3,19},{19,3},{4,20},{20... | collective-permute-start | bytes 3145736 | tf_op jit(solution)/shard_map/ppermute | solution.py:226
  118.4 10.0 %collective-permute-start.8 = (bf16[2,512,512]{2,1,0:T(8,128)(2,1)}, bf16[2,512,512]{2,1,0:T(8,128)(2,1)}, u32[]{:S(2)}, u32[]{:S(2)}) collective-permute-start(bf16[2,512,512]{2,1,0:T(8,128)(2,1)} %copy-done.6), channel_id=1, source_target_pairs={{0,16},{16,0},{1,17},{17,1},{2,18},{18,2},{3,19},{19,3},{4,20},{20... | collective-permute-start | bytes 3145736 | tf_op jit(solution)/shard_map/ppermute | solution.py:226
  118.5 9.9 %collective-permute-start.9 = (bf16[2,512,512]{2,1,0:T(8,128)(2,1)}, bf16[2,512,512]{2,1,0:T(8,128)(2,1)}, u32[]{:S(2)}, u32[]{:S(2)}) collective-permute-start(bf16[2,512,512]{2,1,0:T(8,128)(2,1)} %copy-done.10), channel_id=1, source_target_pairs={{0,16},{16,0},{1,17},{17,1},{2,18},{18,2},{3,19},{19,3},{4,20},{20... | collective-permute-start | bytes 3145736 | tf_op jit(solution)/shard_map/ppermute | solution.py:226
  125.6 5.3 %collective-permute-start.10 = (bf16[2,512,512]{2,1,0:T(8,128)(2,1)}, bf16[2,512,512]{2,1,0:T(8,128)(2,1)}, u32[]{:S(2)}, u32[]{:S(2)}) collective-permute-start(bf16[2,512,512]{2,1,0:T(8,128)(2,1)} %pad_maximum_fusion.1.refs_3_), channel_id=1, source_target_pairs={{0,16},{16,0},{1,17},{17,1},{2,18},{18,2},{3,19},{19,3},{4,20},{20... | collective-permute-start | bytes 3145736 | tf_op jit(solution)/shard_map/ppermute | solution.py:226
  162.3 35.1 %all-to-all-start.4 = ((bf16[16,128,512]{2,1,0:T(8,128)(2,1)}), bf16[16,128,512]{2,1,0:T(8,128)(2,1)}, u32[]{:S(2)}, u32[]{:S(2)}) async-start(bf16[16,128,512]{2,1,0:T(8,128)(2,1)} %copy-done.17), calls=%async_computation.5 | async-start | bytes 4194304 | tf_op jit(solution)/shard_map/all_to_all | solution.py:266
  180.5 33.0 %collective-permute-start.11 = (bf16[512,512]{1,0:T(8,128)(2,1)}, bf16[512,512]{1,0:T(8,128)(2,1)}, u32[]{:S(2)}, u32[]{:S(2)}) collective-permute-start(bf16[512,512]{1,0:T(8,128)(2,1)} %shard_map.175), channel_id=1, source_target_pairs={{0,8},{8,0},{1,9},{9,1},{2,10},{10,2},{3,11},{11,3},{4,12},{12,4},... | collective-permute-start | bytes 1572872 | tf_op jit(solution)/shard_map/ppermute | solution.py:279
  208.9 4.6 %copy-start.23 = (bf16[512,512]{1,0:T(8,128)(2,1)S(1)}, bf16[512,512]{1,0:T(8,128)(2,1)}, u32[]{:S(2)}) copy-start(bf16[512,512]{1,0:T(8,128)(2,1)} %copy-done.22) | copy-start | bytes 1572868
  (20 other events, 26.8 us)
Sparse Core Ops, SparseCore 0:
  9.8 58.6 all-gather.2
  143.9 51.2 reduce-scatter.1

commit v2 on v1

v2 whole, which is shorter than its diff:
```python
import functools

import jax
import jax.numpy as jnp
from jax import lax
from jax.experimental import pallas as pl
from jax.experimental.pallas import tpu as pltpu
from jax.sharding import Mesh
from jax.sharding import PartitionSpec as P

ADAM_STEP = 10

adapter_scale = 0.5
beta_one = 0.9
beta_two = 0.999
adam_eps = 1e-08
weight_decay = 0.01
learn_rate = 0.001

VMEM = pl.BlockSpec(memory_space=pltpu.VMEM)
SMEM = pl.BlockSpec(memory_space=pltpu.SMEM)
ADAPTER = ("xl", "y", "c")
TENSOR = ("xh", "z")
NT = (((1,), (1,)), ((), ()))
TN = (((0,), (0,)), ((), ()))
NN = (((1,), (0,)), ((), ()))


def dot(a, b, dims):
    return lax.dot_general(a, b, dims, preferred_element_type=jnp.float32)


def call(kernel, out_shape, args, scalars, flops, moved, limit=40, scratch=()):
    return pl.pallas_call(
        kernel,
        out_shape=out_shape,
        in_specs=[SMEM] * len(scalars) + [VMEM] * len(args),
        out_specs=jax.tree.map(lambda _: VMEM, out_shape),
        scratch_shapes=list(scratch),
        compiler_params=pltpu.CompilerParams(vmem_limit_bytes=limit * 2**20),
        cost_estimate=pl.CostEstimate(flops=flops, bytes_accessed=moved, transcendentals=0),
    )(*scalars, *args)


def decoupled_adam(parameter, moment, second, gradient):
    moment_new = beta_one * moment + (1.0 - beta_one) * gradient
    second_new = beta_two * second + (1.0 - beta_two) * gradient * gradient
    bias_first = 1.0 - beta_one**ADAM_STEP
    bias_second = 1.0 - beta_two**ADAM_STEP
    update = (
        moment_new / bias_first / (jnp.sqrt(second_new / bias_second) + adam_eps)
        + weight_decay * parameter
    )
    return (parameter - learn_rate * update, moment_new, second_new)


def select_kernel(slot_ref, mine_ref, theirs_ref, send_ref):
    held = mine_ref.shape[0]

    @pl.loop(0, send_ref.shape[0] // 2)
    def _(peer):
        for side, table in enumerate((mine_ref, theirs_ref)):
            at = 2 * peer + side
            send_ref[at] = table[jnp.clip(slot_ref[at], 0, held - 1)]


def low_kernel(owner_ref, x_ref, dy_ref, weight_ref, low_ref):
    tiles = owner_ref.shape[0]
    height = x_ref.shape[0] // tiles
    rank = weight_ref.shape[1] // 2
    for j in range(tiles):
        rows = pl.ds(j * height, height)
        weight = weight_ref[owner_ref[j]]
        fwd = dot(x_ref[rows], weight, NT)
        bwd = dot(dy_ref[rows], weight, NT)
        lane = lax.broadcasted_iota(jnp.int32, fwd.shape, 1)
        low_ref[rows] = jnp.where(lane < rank, fwd, bwd).astype(jnp.bfloat16)


def grad_kernel(owner_ref, low_ref, x_ref, dy_ref, weight_ref, send_ref, out_ref, back_ref):
    tiles = owner_ref.shape[0]
    height = x_ref.shape[0] // tiles
    rank = weight_ref.shape[1] // 2
    send_ref[...] = jnp.zeros_like(send_ref)
    for j in range(tiles):
        rows = pl.ds(j * height, height)
        owner = owner_ref[j]
        weight = weight_ref[owner]
        low = low_ref[rows]
        fwd, bwd = low[:, :rank], low[:, rank:]
        out_ref[rows] = (adapter_scale * dot(fwd, weight[rank:], NN)).astype(jnp.bfloat16)
        back_ref[rows] = (adapter_scale * dot(bwd, weight[:rank], NN)).astype(jnp.bfloat16)
        up_part = dot(low, dy_ref[rows], TN)[:rank]
        down_part = dot(low, x_ref[rows], TN)[rank:]
        part = jnp.concatenate([down_part, up_part], axis=0)
        send_ref[owner] = (adapter_scale * part).astype(jnp.bfloat16)


def collect_kernel(slot_ref, part_ref, mine_ref, theirs_ref, acc):
    held = mine_ref.shape[0]
    acc[...] = jnp.zeros_like(acc)

    @pl.loop(0, part_ref.shape[0] // 2)
    def _(peer):
        for side in range(2):
            at = 2 * peer + side
            slot = slot_ref[at]

            @pl.when((slot >= 0) & (slot < held))
            def _(at=at, side=side, slot=slot):
                acc[side, slot] += part_ref[at].astype(jnp.float32)

    mine_ref[...] = acc[0]
    theirs_ref[...] = acc[1].astype(jnp.bfloat16)


def adam_kernel(mine, theirs, pd, pu, md, vd, mu, vu, npd, npu, nmd, nvd, nmu, nvu):
    held, rank, _ = pd.shape
    for k in range(held):
        grad = mine[k] + theirs[k].astype(jnp.float32)
        npd[k], nmd[k], nvd[k] = decoupled_adam(pd[k], md[k], vd[k], grad[:rank])
        npu[k], nmu[k], nvu[k] = decoupled_adam(pu[k], mu[k], vu[k], grad[rank:])


def back_kernel(at_ref, *refs):
    gradients, weights, out_ref = refs[:4], refs[4:-1], refs[-1]
    for i, weight in enumerate(weights):
        for row in range(2):
            total = dot(gradients[2 * row][...], weight[0], NT)
            total += dot(gradients[2 * row + 1][...], weight[1], NT)
            out_ref[at_ref[i], row] = total.astype(jnp.bfloat16)


def forward_kernel(at_ref, x_ref, *refs, row):
    weights, out_ref = refs[:-2], refs[-2:]
    for j, out in enumerate(out_ref):
        total = dot(x_ref[at_ref[0], row], weights[0][j], NN)
        for i, weight in enumerate(weights[1:], 1):
            total += dot(x_ref[at_ref[i], row], weight[j], NN)
        out[...] = total.astype(out.dtype)


def per_device(
    tokens,
    cotangent,
    frozen_weight,
    adapter_per_tile,
    tile_token_length,
    adapter_down_weight,
    adapter_up_weight,
    down_first_moment,
    down_second_moment,
    up_first_moment,
    up_second_moment,
):
    bf16, f32 = jnp.bfloat16, jnp.float32
    tok_rows, width = tokens.shape
    tile_count = adapter_per_tile.shape[1]
    tile_rows = tok_rows // tile_count
    held, rank, _ = adapter_down_weight.shape
    owners = lax.axis_size(ADAPTER)
    planes = lax.axis_size("z")
    ys = lax.axis_size("y")
    xl, y, c, xh = (lax.axis_index(n) for n in ("xl", "y", "c", "xh"))

    swap = [(0, 1), (1, 0)]
    plane = ("y", "c")
    adapters_mine = jnp.concatenate([adapter_down_weight, adapter_up_weight], axis=1).astype(bf16)
    adapters_theirs = lax.ppermute(adapters_mine, "xl", swap)
    adapters_here = adapter_per_tile[0]
    owner = adapters_here // held
    sites = owners // 2
    owner_of = owner % sites * 2 + (owner // sites != xl).astype(jnp.int32)
    chosen = owner_of[None, :] == jnp.arange(owners, dtype=jnp.int32)[:, None]
    asked = jnp.sum(jnp.where(chosen, adapters_here[None, :] % held - held, 0), axis=1) + held
    slots = lax.all_to_all(
        asked.reshape(sites, 2, 1), plane, split_axis=0, concat_axis=0, tiled=True
    ).reshape(owners)

    cross = [(i, 3 - i) for i in range(4)]
    half = width // 2
    own_half = lax.dynamic_slice_in_dim(tokens, xl * half, half, 1)
    other_half = lax.dynamic_slice_in_dim(tokens, (1 - xl) * half, half, 1)
    got_half = lax.ppermute(other_half, "xl", swap)

    got_half, adapters_theirs, slots = lax.optimization_barrier(
        (got_half, adapters_theirs, slots)
    )
    x_all = lax.all_gather(jnp.stack([own_half, got_half]), "z", axis=0)

    place = [0, 2, 1, 3]
    later, lengths, _ = lax.optimization_barrier((xh, tile_token_length[0], slots))
    keep = lax.dynamic_slice_in_dim(frozen_weight, later * half, half, 0)
    give = lax.dynamic_slice_in_dim(frozen_weight, (1 - later) * half, half, 0)
    first = lax.ppermute(
        give,
        ("xl", "xh"),
        [(place[0], place[1]), (place[1], place[3]), (place[3], place[2]), (place[2], place[0])],
    )
    second = lax.ppermute(keep, ("xl", "xh"), [(place[1], place[2]), (place[2], place[1])])
    position = jnp.arange(tile_rows, dtype=jnp.int32)
    kept = position[None, :] < lengths[:, None]
    dy = jnp.where(
        kept[:, :, None],
        cotangent.reshape(tile_count, tile_rows, width),
        jnp.zeros((), bf16),
    ).reshape(tok_rows, width)

    dy_x = lax.ppermute(dy, "xl", swap)
    dy_h = lax.ppermute(dy, "xh", swap)
    dy_d = lax.ppermute(dy, ("xl", "xh"), cross)

    sent = call(
        select_kernel,
        jax.ShapeDtypeStruct((owners, 2 * rank, width), bf16),
        [adapters_mine, adapters_theirs],
        [slots],
        0,
        3 * 2**20,
    )

    def exchange(blocks):
        moved = lax.all_to_all(
            blocks.reshape(sites, 4 * rank, width), plane, split_axis=0, concat_axis=0, tiled=True
        )
        return moved.reshape(owners, 2 * rank, width)

    tile_weights = exchange(sent)
    side, _ = lax.optimization_barrier((xl, tile_weights[0, 0, :1]))
    left = side == 0
    other = jnp.where(xl == xh, keep, second)
    here = jnp.stack([jnp.where(left, other, first), jnp.where(left, first, other)])

    up_ring = [(i, (i + 1) % ys) for i in range(ys)]
    down_ring = [(i, (i - 1) % ys) for i in range(ys)]
    below = lax.ppermute(here, "y", up_ring)
    above = lax.ppermute(here, "y", down_ring)
    low_part = call(
        low_kernel,
        jax.ShapeDtypeStruct((tok_rows, 2 * rank), bf16),
        [tokens, dy, tile_weights],
        [owner_of],
        8 * tok_rows * width * rank,
        3 * 2**20,
    )

    peers = lax.axis_size(TENSOR)
    share = tok_rows // peers

    def trade(blocks):
        return lax.all_to_all(blocks, TENSOR, split_axis=0, concat_axis=0, tiled=True)

    terms = trade(low_part.reshape(peers, share, 2 * rank))
    below, above, terms = lax.optimization_barrier((below, above, terms))
    far = jnp.stack(
        [lax.ppermute(below[0], "y", up_ring), lax.ppermute(above[1], "y", down_ring)]
    )
    low_share = jnp.sum(terms.astype(f32), axis=0).astype(bf16)
    low = trade(jnp.broadcast_to(low_share[None], (peers, share, 2 * rank)))
    low = low.reshape(tok_rows, 2 * rank)
    far, low = lax.optimization_barrier((far, low))
    mine = [here, below, above, far]
    weights = mine + [lax.ppermute(w, "c", swap) for w in mine]
    steps = [0, ys - 1, 1, 2]
    at = jnp.stack(
        [2 * ((y + s) % ys) + c for s in steps] + [2 * ((y + s) % ys) + 1 - c for s in steps]
    ).astype(jnp.int32)

    big = 2 * tok_rows * planes * width * half
    same = xh == 0
    gradients = [
        jnp.where(same, dy, dy_h),
        jnp.where(same, dy_h, dy),
        jnp.where(same, dy_x, dy_d),
        jnp.where(same, dy_d, dy_x),
    ]
    parts = call(
        back_kernel,
        jax.ShapeDtypeStruct((planes, 2, tok_rows, half), bf16),
        [*gradients, *weights],
        [at],
        4 * big,
        13 * 2**20,
    )
    sums = lax.psum_scatter(parts, "z", scatter_dimension=0)
    sum_own, sum_got = sums[0], sums[1]
    sum_back = lax.ppermute(sum_got, "xl", swap)
    input_sum = jnp.concatenate(
        [jnp.where(left, sum_own, sum_back), jnp.where(left, sum_back, sum_own)], axis=1
    )

    grads_sent, lora_out, lora_grad = call(
        grad_kernel,
        (
            jax.ShapeDtypeStruct((owners, 2 * rank, width), bf16),
            jax.ShapeDtypeStruct((tok_rows, width), bf16),
            jax.ShapeDtypeStruct((tok_rows, width), bf16),
        ),
        [low, tokens, dy, tile_weights],
        [owner_of],
        16 * tok_rows * width * rank,
        6 * 2**20,
    )

    x_all, grads_sent, lora_out = lax.optimization_barrier((x_all, grads_sent, lora_out))
    grad_parts = exchange(grads_sent)
    block = jax.ShapeDtypeStruct((tok_rows, width), bf16)
    forward = [
        call(
            functools.partial(forward_kernel, row=row),
            (block, block),
            [x_all, *weights],
            [at],
            2 * big,
            8 * 2**20,
        )
        for row in (1, 0)
    ]
    (got_a, got_b), (own_a, own_b) = forward
    from_x = lax.ppermute(jnp.where(same, got_a, got_b), "xl", swap)
    from_d = lax.ppermute(jnp.where(same, got_b, got_a), ("xl", "xh"), cross)
    from_h = lax.ppermute(jnp.where(same, own_b, own_a), "xh", swap)
    out_mine = jnp.where(same, own_a, own_b).astype(f32)
    out_mine += from_x.astype(f32) + from_d.astype(f32) + from_h.astype(f32)

    lanes = 128
    state = (
        adapter_down_weight,
        adapter_up_weight,
        down_first_moment,
        down_second_moment,
        up_first_moment,
        up_second_moment,
    )
    state_spec = pl.BlockSpec((held, rank, lanes), lambda i: (0, 0, i))
    grad_spec = pl.BlockSpec((held, 2 * rank, lanes), lambda i: (0, 0, i))
    grad_shape = (held, 2 * rank, width)
    grad_mine, grad_theirs = pl.pallas_call(
        collect_kernel,
        grid=(width // lanes,),
        out_shape=[
            jax.ShapeDtypeStruct(grad_shape, f32),
            jax.ShapeDtypeStruct(grad_shape, bf16),
        ],
        in_specs=[SMEM, pl.BlockSpec((owners, 2 * rank, lanes), lambda i: (0, 0, i))],
        out_specs=[grad_spec] * 2,
        scratch_shapes=[pltpu.VMEM((2, held, 2 * rank, lanes), f32)],
        compiler_params=pltpu.CompilerParams(vmem_limit_bytes=24 * 2**20),
        cost_estimate=pl.CostEstimate(
            flops=2 * owners * rank * width, bytes_accessed=4 * 2**20, transcendentals=0
        ),
    )(slots, grad_parts)
    fresh = pl.pallas_call(
        adam_kernel,
        grid=(width // lanes,),
        out_shape=[jax.ShapeDtypeStruct(adapter_down_weight.shape, f32)] * 6,
        in_specs=[grad_spec] * 2 + [state_spec] * 6,
        out_specs=[state_spec] * 6,
        compiler_params=pltpu.CompilerParams(vmem_limit_bytes=60 * 2**20),
        cost_estimate=pl.CostEstimate(
            flops=60 * held * rank * width, bytes_accessed=8 * 2**20, transcendentals=0
        ),
    )(grad_mine, lax.ppermute(grad_theirs, "xl", swap), *state)

    output = (out_mine + lora_out.astype(f32)).astype(bf16)
    token_gradient = (input_sum.astype(f32) + lora_grad.astype(f32)).astype(bf16)
    return (output, token_gradient, *fresh)


def solution(mesh):
    split = Mesh(mesh.devices.reshape(2, 4, 2, 2, 8), ("xl", "y", "c", "xh", "z"))
    matrix = P(ADAPTER, TENSOR)
    table = P(ADAPTER, None)
    state = P(ADAPTER, None, TENSOR)
    return jax.shard_map(
        per_device,
        mesh=split,
        in_specs=(matrix,) * 3 + (table,) * 2 + (state,) * 6,
        out_specs=(matrix,) * 2 + (state,) * 6,
        check_vma=False,
    )
```

time: 227 us -> 195 us (0.86)
  waiting for transfers between devices: 84.1 us -> 49.8 us
  starting transfers between devices: 46.3 us -> 54.3 us
  local copies, waits for them, and re-layouts: 27.2 us -> 24.6 us
  blocking collectives: 12.6 us -> 10.3 us
    ppermute x1, waiting for transfers between devices: 45.9 us -> 0.01 us  [per_device(): below = lax.ppermute(here, 'y', up_ring)]
    ppermute x4 -> x12, waiting for transfers between devices: 0.01 us -> 11.3 us  [the longest x1 6.82 us: per_device(): lax.ppermute(give, ('xl', 'xh'), [(place[0], place[1]), (place[1], place[...]
    reduce_scatter x1, waiting for transfers between devices: 0.01 us -> 7.74 us  [per_device(): sums = lax.psum_scatter(parts, 'z', scatter_dimension=0)]
    unnamed x52 -> x50, local copies, waits for them, and re-layouts: 24.6 us -> 18 us
    select_n x1 -> x5, other arithmetic: 0.01 us -> 4.39 us  [the longest x1 1.27 us: per_device(): jnp.where(same, dy_d, dy_x)]
    all_to_all x4, waiting for transfers between devices: 35 us -> 30.7 us  [the longest x2 19.8 us: exchange(): lax.all_to_all(blocks.reshape(sites, 4 * rank, width), plane, split_axis=...]
    pallas_call x6, Pallas kernels: 21.8 us -> 17.7 us  [call(): pl.pallas_call(kernel, out_shape=out_shape, in_specs=[SMEM] * len(scalars...]
    ppermute x4, starting transfers between devices: 4.88 us -> 8.91 us  [per_device(): weights = mine + [lax.ppermute(w, 'c', swap) for w in mine]]
  transfers between devices with their start and end apart: 18 -> 26, of which waited for: 5 -> 8; matrix products, arithmetic and copies ran while one was open for 6% -> 9% of each run, Pallas kernels for 12% -> 13%
where the time goes in v2:
time: 195 us; the launch traced here: 193 us
  starting transfers between devices  54.3 us (28%)
  waiting for transfers between devices  49.8 us (26%)
  Pallas kernels  25.8 us (13%)
  local copies, waits for them, and re-layouts  24.6 us (13%)
  between operations  14.5 us (7%)
  other arithmetic  14.1 us (7%)
  blocking collectives  10.3 us (5%)
    all_to_all x2, waiting for transfers between devices, exchange(): lax.all_to_all(blocks.reshape(sites, 4 * rank, width), plane, split_axis=...  19.8 us
    unnamed x50, local copies, waits for them, and re-layouts  18 us
    pallas_call x6, Pallas kernels, call(): pl.pallas_call(kernel, out_shape=out_shape, in_specs=[SMEM] * len(scalars...  17.7 us
    all_to_all x2, starting transfers between devices, trade(): lax.all_to_all(blocks, TENSOR, split_axis=0, concat_axis=0, tiled=True)  16.9 us
    all_to_all x2, starting transfers between devices, exchange(): lax.all_to_all(blocks.reshape(sites, 4 * rank, width), plane, split_axis=...  11.8 us
    all_to_all x2, waiting for transfers between devices, trade(): lax.all_to_all(blocks, TENSOR, split_axis=0, concat_axis=0, tiled=True)  10.9 us
    all_to_all x1, blocking collectives, per_device(): lax.all_to_all(asked.reshape(sites, 2, 1), plane, split_axis=0, concat_ax...  10.3 us
    ppermute x4, starting transfers between devices, per_device(): weights = mine + [lax.ppermute(w, 'c', swap) for w in mine]  8.91 us
  transfers between devices with their start and end apart: 26, of which 8 were waited for; matrix products, arithmetic and copies ran while one was open for 9% of the time, Pallas kernels for 13%

profile of v2, /device:TPU:1, one launch (start us, length us, event | category | flops | bytes accessed | tf_op | source)
XLA Modules:
  0.0 193.3 jit_solution(10665939228267570209)
XLA Ops:
  8.4 2.1 %collective-permute-start = (bf16[512,256]{1,0:T(8,128)(2,1)S(1)}, bf16[512,256]{1,0:T(8,128)(2,1)S(1)}, u32[]{:S(2)}, u32[]{:S(2)}) collective-permute-start(bf16[512,256]{1,0:T(8,128)(2,1)S(1)} %get-tuple-element.77), channel_id=1, source_target_pairs={{0,128},{128,0},{1,129},{129,1},{2,130},{130,2},{3,131},{131,3},{4... | collective-permute-start | bytes 786440 | tf_op jit(solution)/shard_map/ppermute | solution.py:184
  12.0 10.3 %all_to_all.25 = s32[8,2,1]{1,2,0:T(1,128)S(1)} all-to-all(s32[8,2,1]{1,2,0:T(1,128)S(1)} %bitcast.63), channel_id=1, replica_groups=mesh['xl'=2,'y'=4,'c'=2,'xh'=2,'z'=8] {'y','c'}, dimensions={0} | all-to-all | bytes 128 | tf_op jit(solution)/shard_map/all_to_all | solution.py:176
  23.5 2.9 %collective-permute-done.1.theirs_ref = bf16[4,128,512]{2,1,0:T(8,128)(2,1)S(1)} collective-permute-done((bf16[4,128,512]{2,1,0:T(8,128)(2,1)S(1)}, bf16[4,128,512]{2,1,0:T(8,128)(2,1)S(1)}, u32[]{:S(2)}, u32[]{:S(2)}) %collective-permute-start.1) | collective-permute-done | bytes 524320 | tf_op jit(solution)/shard_map/ppermute | solution.py:169
  29.4 7.3 %all-to-all-start.1 = ((bf16[8,256,512]{2,1,0:T(8,128)(2,1)}), bf16[8,256,512]{2,1,0:T(8,128)(2,1)S(1)}, u32[]{:S(2)}, u32[]{:S(2)}) async-start(bf16[8,256,512]{2,1,0:T(8,128)(2,1)} %bitcast.59), calls=%async_computation.1 | async-start | bytes 4194304 | tf_op jit(solution)/shard_map/all_to_all | solution.py:223
  40.5 6.8 %collective-permute-done.3 = bf16[256,512]{1,0:T(8,128)(2,1)S(1)} collective-permute-done((bf16[256,512]{1,0:T(8,128)(2,1)S(1)}, bf16[256,512]{1,0:T(8,128)(2,1)S(1)}, u32[]{:S(2)}, u32[]{:S(2)}) %collective-permute-start.3) | collective-permute-done | bytes 262176 | tf_op jit(solution)/shard_map/ppermute | solution.py:195
  52.2 10.8 %all-to-all-done.1 = bf16[8,256,512]{2,1,0:T(8,128)(2,1)S(1)} async-done(((bf16[8,256,512]{2,1,0:T(8,128)(2,1)}), bf16[8,256,512]{2,1,0:T(8,128)(2,1)S(1)}, u32[]{:S(2)}, u32[]{:S(2)}) %all-to-all-start.1) | async-done | bytes 2097184 | tf_op jit(solution)/shard_map/all_to_all | solution.py:223
  65.7 10.8 %all-to-all-start.2 = ((bf16[16,32,128]{2,1,0:T(8,128)(2,1)}), bf16[16,32,128]{2,1,0:T(8,128)(2,1)S(1)}, u32[]{:S(2)}, u32[]{:S(2)}) async-start(bf16[16,32,128]{2,1,0:T(8,128)(2,1)} %bitcast.21), calls=%async_computation.2 | async-start | bytes 262144 | tf_op jit(solution)/shard_map/all_to_all | solution.py:251
  76.5 2.6 %collective-permute-start.17 = (bf16[512,512]{1,0:T(8,128)(2,1)}, bf16[512,512]{1,0:T(8,128)(2,1)}, u32[]{:S(2)}, u32[]{:S(2)}) collective-permute-start(bf16[512,512]{1,0:T(8,128)(2,1)} %broadcast_select_fusion.dy_ref), channel_id=1, source_target_pairs={{0,136},{8,128},{128,8},{136,0},{1,137},{9,129},{129,9},{137,1},{2... | collective-permute-start | bytes 1572872 | tf_op jit(solution)/shard_map/ppermute | solution.py:211
  79.1 7.0 %all-to-all-done.2 = bf16[16,32,128]{2,1,0:T(8,128)(2,1)S(1)} async-done(((bf16[16,32,128]{2,1,0:T(8,128)(2,1)}), bf16[16,32,128]{2,1,0:T(8,128)(2,1)S(1)}, u32[]{:S(2)}, u32[]{:S(2)}) %all-to-all-start.2) | async-done | bytes 131104 | tf_op jit(solution)/shard_map/all_to_all | solution.py:251
  90.9 6.1 %all-to-all-start.3 = ((bf16[16,32,128]{2,1,0:T(8,128)(2,1)}), bf16[16,32,128]{2,1,0:T(8,128)(2,1)S(1)}, u32[]{:S(2)}, u32[]{:S(2)}) async-start(bf16[16,32,128]{2,1,0:T(8,128)(2,1)} %broadcast_in_dim.42), calls=%async_computation.3 | async-start | bytes 262144 | tf_op jit(solution)/shard_map/all_to_all | solution.py:251
  97.2 3.8 %collective-permute-start.8 = (bf16[2,256,512]{2,1,0:T(8,128)(2,1)S(1)}, bf16[2,256,512]{2,1,0:T(8,128)(2,1)}, u32[]{:S(2)}, u32[]{:S(2)}) collective-permute-start(bf16[2,256,512]{2,1,0:T(8,128)(2,1)S(1)} %pad_maximum_fusion.2.refs_0_.refs_4_), channel_id=1, source_target_pairs={{0,16},{16,0},{1,17},{17,1},{2,18},{18,2},{3,19},{19,3},{4,20},{20... | collective-permute-start | bytes 1572872 | tf_op jit(solution)/shard_map/ppermute | solution.py:263
  102.2 3.9 %all-to-all-done.3 = bf16[16,32,128]{2,1,0:T(8,128)(2,1)S(1)} async-done(((bf16[16,32,128]{2,1,0:T(8,128)(2,1)}), bf16[16,32,128]{2,1,0:T(8,128)(2,1)S(1)}, u32[]{:S(2)}, u32[]{:S(2)}) %all-to-all-start.3) | async-done | bytes 131104 | tf_op jit(solution)/shard_map/all_to_all | solution.py:251
  106.0 4.7 %collective-permute-start.10 = (bf16[2,256,512]{2,1,0:T(8,128)(2,1)}, bf16[2,256,512]{2,1,0:T(8,128)(2,1)S(1)}, u32[]{:S(2)}, u32[]{:S(2)}) collective-permute-start(bf16[2,256,512]{2,1,0:T(8,128)(2,1)} %collective-permute-done.5.refs_2_.refs_6_), channel_id=1, source_target_pairs={{0,16},{16,0},{1,17},{17,1},{2,18},{18,2},{3,19},{19,3},{4,20},{20... | collective-permute-start | bytes 1572872 | tf_op jit(solution)/shard_map/ppermute | solution.py:263
  113.6 6.2 %shard_map.175 = bf16[8,2,512,256]{3,2,1,0:T(8,128)(2,1)S(1)} custom-call(s32[8]{0:T(128)S(1)} %stack.62.at_ref, bf16[512,512]{1,0:T(8,128)(2,1)S(1)} %get-tuple-element.67.refs_0_, bf16[512,512]{1,0:T(8,128)(2,1)S(1)} %get-tuple-element.66.refs_1_, bf16[512,512]{1,0:T(8,128)(2,1)S(1)} %get-tuple-element.65.refs_2_, ...), custom_call_target="tpu_custom_call" | custom-call | flops 4294967296 | bytes 13631488 | tf_op jit(solution)/shard_map/pallas_call | solution.py:34
  129.9 4.5 %all-to-all-start.4 = ((bf16[8,256,512]{2,1,0:T(8,128)(2,1)}), bf16[8,256,512]{2,1,0:T(8,128)(2,1)}, u32[]{:S(2)}, u32[]{:S(2)}) async-start(bf16[8,256,512]{2,1,0:T(8,128)(2,1)} %bitcast.60), calls=%async_computation.5 | async-start | bytes 4194304 | tf_op jit(solution)/shard_map/all_to_all | solution.py:223
  134.4 2.2 %copy-done = bf16[16,512,256]{2,1,0:T(8,128)(2,1)S(1)} copy-done((bf16[16,512,256]{2,1,0:T(8,128)(2,1)S(1)}, bf16[16,512,256]{2,1,0:T(8,128)(2,1)}, u32[]{:S(2)}) %copy-start) | copy-done | bytes 4194328
  138.7 3.9 %shard_map.173 = (bf16[512,512]{1,0:T(8,128)(2,1)S(1)}, bf16[512,512]{1,0:T(8,128)(2,1)S(1)}) custom-call(s32[8]{0:T(128)S(1)} %stack.62.at_ref, bf16[8,2,512,256]{3,2,1,0:T(8,128)(2,1)S(1)} %bitcast.57, bf16[2,256,512]{2,1,0:T(8,128)(2,1)S(1)} %pad_maximum_fusion.2.refs_0_.refs_4_, bf16[2,256,512]{2,1,0:T(8,128)(2,1)} %collective-permute-done.4.refs_1_.refs_5_, ...), custom_call_target="tpu_custom_call" | custom-call | flops 2147483648 | bytes 8388608 | tf_op jit(solution)/shard_map/pallas_call | solution.py:34
  144.8 3.9 %shard_map.174 = (bf16[512,512]{1,0:T(8,128)(2,1)S(1)}, bf16[512,512]{1,0:T(8,128)(2,1)S(1)}) custom-call(s32[8]{0:T(128)S(1)} %stack.62.at_ref, bf16[8,2,512,256]{3,2,1,0:T(8,128)(2,1)S(1)} %bitcast.58, bf16[2,256,512]{2,1,0:T(8,128)(2,1)S(1)} %pad_maximum_fusion.2.refs_0_.refs_4_, bf16[2,256,512]{2,1,0:T(8,128)(2,1)} %collective-permute-done.4.refs_1_.refs_5_, ...), custom_call_target="tpu_custom_call" | custom-call | flops 2147483648 | bytes 8388608 | tf_op jit(solution)/shard_map/pallas_call | solution.py:34
  149.7 2.1 %collective-permute-start.13 = (bf16[512,512]{1,0:T(8,128)(2,1)}, bf16[512,512]{1,0:T(8,128)(2,1)}, u32[]{:S(2)}, u32[]{:S(2)}) collective-permute-start(bf16[512,512]{1,0:T(8,128)(2,1)} %get-tuple-element.69), channel_id=1, source_target_pairs={{0,136},{8,128},{128,8},{136,0},{1,137},{9,129},{129,9},{137,1},{2... | collective-permute-start | bytes 1572872 | tf_op jit(solution)/shard_map/ppermute | solution.py:321
  151.9 9.0 %all-to-all-done.4 = bf16[8,256,512]{2,1,0:T(8,128)(2,1)} async-done(((bf16[8,256,512]{2,1,0:T(8,128)(2,1)}), bf16[8,256,512]{2,1,0:T(8,128)(2,1)}, u32[]{:S(2)}, u32[]{:S(2)}) %all-to-all-start.4) | async-done | bytes 2097184 | tf_op jit(solution)/shard_map/all_to_all | solution.py:223
  160.8 3.2 %shard_map.176 = (f32[4,128,512]{2,1,0:T(8,128)S(1)}, bf16[4,128,512]{2,1,0:T(8,128)(2,1)S(1)}) custom-call(s32[16]{0:T(128)S(1)} %reshape.78.slot_ref, bf16[16,128,512]{2,1,0:T(8,128)(2,1)} %bitcast.30.part_ref), custom_call_target="tpu_custom_call" | custom-call | flops 1048576 | bytes 4194304 | tf_op jit(solution)/shard_map/pallas_call | solution.py:338
  165.4 7.7 %reduce-scatter.2.cloned.1.call-done = bf16[1,2,512,256]{3,2,1,0:T(8,128)(2,1)} async-done(((bf16[8,2,512,256]{3,2,1,0:T(8,128)(2,1)}), bf16[1,2,512,256]{3,2,1,0:T(8,128)(2,1)}) %reduce-scatter.2.cloned.1.call-update) | async-done | bytes 524304 | tf_op jit(solution)/shard_map/reduce_scatter | solution.py:285
  175.4 2.7 %add_convert_fusion.1 = bf16[512,512]{1,0:T(8,128)(2,1)} fusion(bf16[512,512]{1,0:T(8,128)(2,1)} %copy-done.18, bf16[512,512]{1,0:T(8,128)(2,1)} %collective-permute-done.14, bf16[512,512]{1,0:T(8,128)(2,1)} %collective-permute-done.13, bf16[512,512]{1,0:T(8,128)(2,1)} %collective-permute-done.12, bf16[512,512]{1,0:T(8,128)(2,1)S(1)} %copy-done.13, ...), kind=kLoop, calls=%fused_computation.1 | loop fusion | flops 2883584 | bytes 3670017 | tf_op jit(solution)/shard_map/convert_element_type | solution.py:365
  180.5 4.9 %shard_map.177 = (f32[4,64,512]{2,1,0:T(8,128)}, f32[4,64,512]{2,1,0:T(8,128)}, f32[4,64,512]{2,1,0:T(8,128)}, f32[4,64,512]{2,1,0:T(8,128)}, f32[4,64,512]{2,1,0:T(8,128)}, /*index=5*/f32[4,64,512]{2,1,0:T(8,128)}) custom-call(f32[4,128,512]{2,1,0:T(8,128)} %copy-done.15, bf16[4,128,512]{2,1,0:T(8,128)(2,1)} %copy-done.21, f32[4,64,512]{2,1,0:T(8,128)} %pd.1, ...), custom_call_target="tpu_custom_call" | custom-call | flops 7864320 | bytes 8388608 | tf_op jit(solution)/shard_map/pallas_call | solution.py:353
  (121 shorter events, 49.3 us)
Async XLA Ops:
  7.2 122.7 %all-gather.3.cloned.1.call-start = ((), (), s32[]{:S(2)}) async-start(), calls=%async_computation.7 | async-start | bytes 4718592 | tf_op jit(solution)/shard_map/all_gather | solution.py:189
  8.4 15.2 %collective-permute-start = (bf16[512,256]{1,0:T(8,128)(2,1)S(1)}, bf16[512,256]{1,0:T(8,128)(2,1)S(1)}, u32[]{:S(2)}, u32[]{:S(2)}) collective-permute-start(bf16[512,256]{1,0:T(8,128)(2,1)S(1)} %get-tuple-element.77), channel_id=1, source_target_pairs={{0,128},{128,0},{1,129},{129,1},{2,130},{130,2},{3,131},{131,3},{4... | collective-permute-start | bytes 786440 | tf_op jit(solution)/shard_map/ppermute | solution.py:184
  11.7 14.8 %collective-permute-start.1 = (bf16[4,128,512]{2,1,0:T(8,128)(2,1)S(1)}, bf16[4,128,512]{2,1,0:T(8,128)(2,1)S(1)}, u32[]{:S(2)}, u32[]{:S(2)}) collective-permute-start(bf16[4,128,512]{2,1,0:T(8,128)(2,1)S(1)} %pad_maximum_fusion.mine_ref), channel_id=1, source_target_pairs={{0,128},{128,0},{1,129},{129,1},{2,130},{130,2},{3,131},{131,3},{4... | collective-permute-start | bytes 1572872 | tf_op jit(solution)/shard_map/ppermute | solution.py:169
  29.4 33.7 %all-to-all-start.1 = ((bf16[8,256,512]{2,1,0:T(8,128)(2,1)}), bf16[8,256,512]{2,1,0:T(8,128)(2,1)S(1)}, u32[]{:S(2)}, u32[]{:S(2)}) async-start(bf16[8,256,512]{2,1,0:T(8,128)(2,1)} %bitcast.59), calls=%async_computation.1 | async-start | bytes 4194304 | tf_op jit(solution)/shard_map/all_to_all | solution.py:223
  37.8 9.5 %collective-permute-start.3 = (bf16[256,512]{1,0:T(8,128)(2,1)S(1)}, bf16[256,512]{1,0:T(8,128)(2,1)S(1)}, u32[]{:S(2)}, u32[]{:S(2)}) collective-permute-start(bf16[256,512]{1,0:T(8,128)(2,1)S(1)} %get-tuple-element.75), channel_id=1, source_target_pairs={{0,128},{128,136},{136,8},{8,0},{1,129},{129,137},{137,9},{9,1},{2... | collective-permute-start | bytes 786440 | tf_op jit(solution)/shard_map/ppermute | solution.py:195
  39.1 8.2 %collective-permute-start.2 = (bf16[256,512]{1,0:T(8,128)(2,1)S(1)}, bf16[256,512]{1,0:T(8,128)(2,1)}, u32[]{:S(2)}, u32[]{:S(2)}) collective-permute-start(bf16[256,512]{1,0:T(8,128)(2,1)S(1)} %get-tuple-element.74), channel_id=1, source_target_pairs={{128,8},{8,128},{129,9},{9,129},{130,10},{10,130},{131,11},{11,131... | collective-permute-start | bytes 786440 | tf_op jit(solution)/shard_map/ppermute | solution.py:200
  47.4 31.7 %collective-permute-start.4 = (bf16[2,256,512]{2,1,0:T(8,128)(2,1)S(1)}, bf16[2,256,512]{2,1,0:T(8,128)(2,1)}, u32[]{:S(2)}, u32[]{:S(2)}) collective-permute-start(bf16[2,256,512]{2,1,0:T(8,128)(2,1)S(1)} %pad_maximum_fusion.2.refs_0_.refs_4_), channel_id=1, source_target_pairs={{0,32},{32,64},{64,96},{96,0},{1,33},{33,65},{65,97},{97,1},{2,34}... | collective-permute-start | bytes 1572872 | tf_op jit(solution)/shard_map/ppermute | solution.py:236
  48.5 30.6 %collective-permute-start.5 = (bf16[2,256,512]{2,1,0:T(8,128)(2,1)S(1)}, bf16[2,256,512]{2,1,0:T(8,128)(2,1)}, u32[]{:S(2)}, u32[]{:S(2)}) collective-permute-start(bf16[2,256,512]{2,1,0:T(8,128)(2,1)S(1)} %pad_maximum_fusion.2.refs_0_.refs_4_), channel_id=1, source_target_pairs={{0,96},{32,0},{64,32},{96,64},{1,97},{33,1},{65,33},{97,65},{2,98}... | collective-permute-start | bytes 1572872 | tf_op jit(solution)/shard_map/ppermute | solution.py:237
  65.7 20.4 %all-to-all-start.2 = ((bf16[16,32,128]{2,1,0:T(8,128)(2,1)}), bf16[16,32,128]{2,1,0:T(8,128)(2,1)S(1)}, u32[]{:S(2)}, u32[]{:S(2)}) async-start(bf16[16,32,128]{2,1,0:T(8,128)(2,1)} %bitcast.21), calls=%async_computation.2 | async-start | bytes 262144 | tf_op jit(solution)/shard_map/all_to_all | solution.py:251
  76.5 29.6 %collective-permute-start.17 = (bf16[512,512]{1,0:T(8,128)(2,1)}, bf16[512,512]{1,0:T(8,128)(2,1)}, u32[]{:S(2)}, u32[]{:S(2)}) collective-permute-start(bf16[512,512]{1,0:T(8,128)(2,1)} %broadcast_select_fusion.dy_ref), channel_id=1, source_target_pairs={{0,136},{8,128},{128,8},{136,0},{1,137},{9,129},{129,9},{137,1},{2... | collective-permute-start | bytes 1572872 | tf_op jit(solution)/shard_map/ppermute | solution.py:211
  79.1 31.7 %collective-permute-start.16 = (bf16[512,512]{1,0:T(8,128)(2,1)}, bf16[512,512]{1,0:T(8,128)(2,1)}, u32[]{:S(2)}, u32[]{:S(2)}) collective-permute-start(bf16[512,512]{1,0:T(8,128)(2,1)} %broadcast_select_fusion.dy_ref), channel_id=1, source_target_pairs={{0,128},{128,0},{1,129},{129,1},{2,130},{130,2},{3,131},{131,3},{4... | collective-permute-start | bytes 1572872 | tf_op jit(solution)/shard_map/ppermute | solution.py:209
  87.1 10.1 %collective-permute-start.7 = (bf16[256,512]{1,0:T(8,128)(2,1)S(1)}, bf16[256,512]{1,0:T(8,128)(2,1)}, u32[]{:S(2)}, u32[]{:S(2)}) collective-permute-start(bf16[256,512]{1,0:T(8,128)(2,1)S(1)} %slice_bitcast_fusion.2), channel_id=1, source_target_pairs={{0,96},{32,0},{64,32},{96,64},{1,97},{33,1},{65,33},{97,65},{2,98}... | collective-permute-start | bytes 786440 | tf_op jit(solution)/shard_map/ppermute | solution.py:256
  89.0 12.0 %collective-permute-start.6 = (bf16[256,512]{1,0:T(8,128)(2,1)S(1)}, bf16[256,512]{1,0:T(8,128)(2,1)}, u32[]{:S(2)}, u32[]{:S(2)}) collective-permute-start(bf16[256,512]{1,0:T(8,128)(2,1)S(1)} %slice_bitcast_fusion.3), channel_id=1, source_target_pairs={{0,32},{32,64},{64,96},{96,0},{1,33},{33,65},{65,97},{97,1},{2,34}... | collective-permute-start | bytes 786440 | tf_op jit(solution)/shard_map/ppermute | solution.py:256
  89.7 22.7 %collective-permute-start.15 = (bf16[512,512]{1,0:T(8,128)(2,1)}, bf16[512,512]{1,0:T(8,128)(2,1)}, u32[]{:S(2)}, u32[]{:S(2)}) collective-permute-start(bf16[512,512]{1,0:T(8,128)(2,1)} %broadcast_select_fusion.dy_ref), channel_id=1, source_target_pairs={{0,8},{8,0},{1,9},{9,1},{2,10},{10,2},{3,11},{11,3},{4,12},{12,4},... | collective-permute-start | bytes 1572872 | tf_op jit(solution)/shard_map/ppermute | solution.py:210
  90.9 15.2 %all-to-all-start.3 = ((bf16[16,32,128]{2,1,0:T(8,128)(2,1)}), bf16[16,32,128]{2,1,0:T(8,128)(2,1)S(1)}, u32[]{:S(2)}, u32[]{:S(2)}) async-start(bf16[16,32,128]{2,1,0:T(8,128)(2,1)} %broadcast_in_dim.42), calls=%async_computation.3 | async-start | bytes 262144 | tf_op jit(solution)/shard_map/all_to_all | solution.py:251
  97.0 76.1 %reduce-scatter.2.cloned.1.call-start = ((), (), s32[]{:S(2)}) async-start(), calls=%async_computation.6 | async-start | bytes 4718592 | tf_op jit(solution)/shard_map/reduce_scatter | solution.py:285
  97.2 16.4 %collective-permute-start.8 = (bf16[2,256,512]{2,1,0:T(8,128)(2,1)S(1)}, bf16[2,256,512]{2,1,0:T(8,128)(2,1)}, u32[]{:S(2)}, u32[]{:S(2)}) collective-permute-start(bf16[2,256,512]{2,1,0:T(8,128)(2,1)S(1)} %pad_maximum_fusion.2.refs_0_.refs_4_), channel_id=1, source_target_pairs={{0,16},{16,0},{1,17},{17,1},{2,18},{18,2},{3,19},{19,3},{4,20},{20... | collective-permute-start | bytes 1572872 | tf_op jit(solution)/shard_map/ppermute | solution.py:263
  101.0 12.6 %collective-permute-start.9 = (bf16[2,256,512]{2,1,0:T(8,128)(2,1)}, bf16[2,256,512]{2,1,0:T(8,128)(2,1)}, u32[]{:S(2)}, u32[]{:S(2)}) collective-permute-start(bf16[2,256,512]{2,1,0:T(8,128)(2,1)} %collective-permute-done.4.refs_1_.refs_5_), channel_id=1, source_target_pairs={{0,16},{16,0},{1,17},{17,1},{2,18},{18,2},{3,19},{19,3},{4,20},{20... | collective-permute-start | bytes 1572872 | tf_op jit(solution)/shard_map/ppermute | solution.py:263
  129.9 30.9 %all-to-all-start.4 = ((bf16[8,256,512]{2,1,0:T(8,128)(2,1)}), bf16[8,256,512]{2,1,0:T(8,128)(2,1)}, u32[]{:S(2)}, u32[]{:S(2)}) async-start(bf16[8,256,512]{2,1,0:T(8,128)(2,1)} %bitcast.60), calls=%async_computation.5 | async-start | bytes 4194304 | tf_op jit(solution)/shard_map/all_to_all | solution.py:223
  144.3 31.1 %collective-permute-start.14 = (bf16[512,512]{1,0:T(8,128)(2,1)}, bf16[512,512]{1,0:T(8,128)(2,1)}, u32[]{:S(2)}, u32[]{:S(2)}) collective-permute-start(bf16[512,512]{1,0:T(8,128)(2,1)} %broadcast_select_fusion.5), channel_id=1, source_target_pairs={{0,8},{8,0},{1,9},{9,1},{2,10},{10,2},{3,11},{11,3},{4,12},{12,4},... | collective-permute-start | bytes 1572872 | tf_op jit(solution)/shard_map/ppermute | solution.py:322
  149.7 25.7 %collective-permute-start.13 = (bf16[512,512]{1,0:T(8,128)(2,1)}, bf16[512,512]{1,0:T(8,128)(2,1)}, u32[]{:S(2)}, u32[]{:S(2)}) collective-permute-start(bf16[512,512]{1,0:T(8,128)(2,1)} %get-tuple-element.69), channel_id=1, source_target_pairs={{0,136},{8,128},{128,8},{136,0},{1,137},{9,129},{129,9},{137,1},{2... | collective-permute-start | bytes 1572872 | tf_op jit(solution)/shard_map/ppermute | solution.py:321
  151.8 23.5 %collective-permute-start.12 = (bf16[512,512]{1,0:T(8,128)(2,1)}, bf16[512,512]{1,0:T(8,128)(2,1)}, u32[]{:S(2)}, u32[]{:S(2)}) collective-permute-start(bf16[512,512]{1,0:T(8,128)(2,1)} %get-tuple-element.68), channel_id=1, source_target_pairs={{0,128},{128,0},{1,129},{129,1},{2,130},{130,2},{3,131},{131,3},{4... | collective-permute-start | bytes 1572872 | tf_op jit(solution)/shard_map/ppermute | solution.py:320
  165.0 14.7 %collective-permute-start.19 = (bf16[4,128,512]{2,1,0:T(8,128)(2,1)S(1)}, bf16[4,128,512]{2,1,0:T(8,128)(2,1)S(1)}, u32[]{:S(2)}, u32[]{:S(2)}) collective-permute-start(bf16[4,128,512]{2,1,0:T(8,128)(2,1)S(1)} %get-tuple-element.57), channel_id=1, source_target_pairs={{0,128},{128,0},{1,129},{129,1},{2,130},{130,2},{3,131},{131,3},{4... | collective-permute-start | bytes 1572872 | tf_op jit(solution)/shard_map/ppermute | solution.py:363
  174.1 11.3 %collective-permute-start.18 = (bf16[512,256]{1,0:T(8,128)(2,1)S(1)}, bf16[512,256]{1,0:T(8,128)(2,1)S(1)}, u32[]{:S(2)}, u32[]{:S(2)}) collective-permute-start(bf16[512,256]{1,0:T(8,128)(2,1)S(1)} %slice_bitcast_fusion), channel_id=1, source_target_pairs={{0,128},{128,0},{1,129},{129,1},{2,130},{130,2},{3,131},{131,3},{4... | collective-permute-start | bytes 786440 | tf_op jit(solution)/shard_map/ppermute | solution.py:287
  (27 other events, 121.8 us)
Sparse Core Ops, SparseCore 0:
  27.4 62.7 all-gather.2
  123.6 49.5 reduce-scatter.1

commit v3 on v2

--- a/solution.py
+++ b/solution.py
@@ -96,38 +96,43 @@
         send_ref[owner] = (adapter_scale * part).astype(jnp.bfloat16)
 
 
-def collect_kernel(slot_ref, part_ref, mine_ref, theirs_ref, acc):
-    held = mine_ref.shape[0]
+def collect(slot_ref, part_ref, acc, side):
+    held = acc.shape[0]
     acc[...] = jnp.zeros_like(acc)
 
     @pl.loop(0, part_ref.shape[0] // 2)
     def _(peer):
-        for side in range(2):
-            at = 2 * peer + side
-            slot = slot_ref[at]
-
-            @pl.when((slot >= 0) & (slot < held))
-            def _(at=at, side=side, slot=slot):
-                acc[side, slot] += part_ref[at].astype(jnp.float32)
-
-    mine_ref[...] = acc[0]
-    theirs_ref[...] = acc[1].astype(jnp.bfloat16)
-
-
-def adam_kernel(mine, theirs, pd, pu, md, vd, mu, vu, npd, npu, nmd, nvd, nmu, nvu):
+        at = 2 * peer + side
+        slot = slot_ref[at]
+
+        @pl.when((slot >= 0) & (slot < held))
+        def _():
+            acc[slot] += part_ref[at].astype(jnp.float32)
+
+
+def collect_kernel(slot_ref, part_ref, theirs_ref, acc):
+    collect(slot_ref, part_ref, acc, 1)
+    theirs_ref[...] = acc[...].astype(jnp.bfloat16)
+
+
+def adam_kernel(
+    slot_ref, part_ref, theirs, pd, pu, md, vd, mu, vu, npd, npu, nmd, nvd, nmu, nvu, acc
+):
     held, rank, _ = pd.shape
+    collect(slot_ref, part_ref, acc, 0)
     for k in range(held):
-        grad = mine[k] + theirs[k].astype(jnp.float32)
+        grad = acc[k] + theirs[k].astype(jnp.float32)
         npd[k], nmd[k], nvd[k] = decoupled_adam(pd[k], md[k], vd[k], grad[:rank])
         npu[k], nmu[k], nvu[k] = decoupled_adam(pu[k], mu[k], vu[k], grad[rank:])
 
 
 def back_kernel(at_ref, *refs):
     gradients, weights, out_ref = refs[:4], refs[4:-1], refs[-1]
+    column = at_ref[len(weights)]
     for i, weight in enumerate(weights):
         for row in range(2):
-            total = dot(gradients[2 * row][...], weight[0], NT)
-            total += dot(gradients[2 * row + 1][...], weight[1], NT)
+            total = dot(gradients[2 * row][...], weight[column], NT)
+            total += dot(gradients[2 * row + 1][...], weight[1 - column], NT)
             out_ref[at_ref[i], row] = total.astype(jnp.bfloat16)
 
 
@@ -235,6 +240,7 @@
     down_ring = [(i, (i - 1) % ys) for i in range(ys)]
     below = lax.ppermute(here, "y", up_ring)
     above = lax.ppermute(here, "y", down_ring)
+    far = lax.ppermute(here, "y", [(i, (i + 2) % ys) for i in range(ys)])
     low_part = call(
         low_kernel,
         jax.ShapeDtypeStruct((tok_rows, 2 * rank), bf16),
@@ -251,33 +257,27 @@
         return lax.all_to_all(blocks, TENSOR, split_axis=0, concat_axis=0, tiled=True)
 
     terms = trade(low_part.reshape(peers, share, 2 * rank))
-    below, above, terms = lax.optimization_barrier((below, above, terms))
-    far = jnp.stack(
-        [lax.ppermute(below[0], "y", up_ring), lax.ppermute(above[1], "y", down_ring)]
-    )
-    low_share = jnp.sum(terms.astype(f32), axis=0).astype(bf16)
-    low = trade(jnp.broadcast_to(low_share[None], (peers, share, 2 * rank)))
-    low = low.reshape(tok_rows, 2 * rank)
-    far, low = lax.optimization_barrier((far, low))
+    here, below, above, _ = lax.optimization_barrier((here, below, above, low_part))
+    far, _ = lax.optimization_barrier((far, terms))
     mine = [here, below, above, far]
     weights = mine + [lax.ppermute(w, "c", swap) for w in mine]
     steps = [0, ys - 1, 1, 2]
     at = jnp.stack(
-        [2 * ((y + s) % ys) + c for s in steps] + [2 * ((y + s) % ys) + 1 - c for s in steps]
+        [2 * ((y + s) % ys) + c for s in steps]
+        + [2 * ((y + s) % ys) + 1 - c for s in steps]
+        + [xh]
     ).astype(jnp.int32)
 
+    low_share = jnp.sum(terms.astype(f32), axis=0).astype(bf16)
+    low = trade(jnp.broadcast_to(low_share[None], (peers, share, 2 * rank)))
+    low = low.reshape(tok_rows, 2 * rank)
+    at, low = lax.optimization_barrier((at, low))
     big = 2 * tok_rows * planes * width * half
     same = xh == 0
-    gradients = [
-        jnp.where(same, dy, dy_h),
-        jnp.where(same, dy_h, dy),
-        jnp.where(same, dy_x, dy_d),
-        jnp.where(same, dy_d, dy_x),
-    ]
     parts = call(
         back_kernel,
         jax.ShapeDtypeStruct((planes, 2, tok_rows, half), bf16),
-        [*gradients, *weights],
+        [dy, dy_h, dy_x, dy_d, *weights],
         [at],
         4 * big,
         13 * 2**20,
@@ -300,6 +300,7 @@
         [owner_of],
         16 * tok_rows * width * rank,
         6 * 2**20,
+        limit=58,
     )
 
     x_all, grads_sent, lora_out = lax.optimization_barrier((x_all, grads_sent, lora_out))
@@ -335,32 +336,32 @@
     state_spec = pl.BlockSpec((held, rank, lanes), lambda i: (0, 0, i))
     grad_spec = pl.BlockSpec((held, 2 * rank, lanes), lambda i: (0, 0, i))
     grad_shape = (held, 2 * rank, width)
-    grad_mine, grad_theirs = pl.pallas_call(
+    part_spec = pl.BlockSpec((owners, 2 * rank, lanes), lambda i: (0, 0, i))
+    acc = pltpu.VMEM((held, 2 * rank, lanes), f32)
+    grad_theirs = pl.pallas_call(
         collect_kernel,
         grid=(width // lanes,),
-        out_shape=[
-            jax.ShapeDtypeStruct(grad_shape, f32),
-            jax.ShapeDtypeStruct(grad_shape, bf16),
-        ],
-        in_specs=[SMEM, pl.BlockSpec((owners, 2 * rank, lanes), lambda i: (0, 0, i))],
-        out_specs=[grad_spec] * 2,
-        scratch_shapes=[pltpu.VMEM((2, held, 2 * rank, lanes), f32)],
+        out_shape=jax.ShapeDtypeStruct(grad_shape, bf16),
+        in_specs=[SMEM, part_spec],
+        out_specs=grad_spec,
+        scratch_shapes=[acc],
         compiler_params=pltpu.CompilerParams(vmem_limit_bytes=24 * 2**20),
         cost_estimate=pl.CostEstimate(
-            flops=2 * owners * rank * width, bytes_accessed=4 * 2**20, transcendentals=0
+            flops=owners * rank * width, bytes_accessed=3 * 2**20, transcendentals=0
         ),
     )(slots, grad_parts)
     fresh = pl.pallas_call(
         adam_kernel,
         grid=(width // lanes,),
         out_shape=[jax.ShapeDtypeStruct(adapter_down_weight.shape, f32)] * 6,
-        in_specs=[grad_spec] * 2 + [state_spec] * 6,
+        in_specs=[SMEM, part_spec, grad_spec] + [state_spec] * 6,
         out_specs=[state_spec] * 6,
+        scratch_shapes=[acc],
         compiler_params=pltpu.CompilerParams(vmem_limit_bytes=60 * 2**20),
         cost_estimate=pl.CostEstimate(
             flops=60 * held * rank * width, bytes_accessed=8 * 2**20, transcendentals=0
         ),
-    )(grad_mine, lax.ppermute(grad_theirs, "xl", swap), *state)
+    )(slots, grad_parts, lax.ppermute(grad_theirs, "xl", swap), *state)
 
     output = (out_mine + lora_out.astype(f32)).astype(bf16)
     token_gradient = (input_sum.astype(f32) + lora_grad.astype(f32)).astype(bf16)

time: 195 us -> 187 us (0.959)
  local copies, waits for them, and re-layouts: 24.6 us -> 11 us
  Pallas kernels: 25.8 us -> 31.5 us
  starting transfers between devices: 54.3 us -> 58.4 us
  other arithmetic: 14.1 us -> 11.6 us
    unnamed x50 -> x36, local copies, waits for them, and re-layouts: 18 us -> 6.39 us
    pallas_call x6, Pallas kernels: 17.7 us -> 23.4 us  [call(): pl.pallas_call(kernel, out_shape=out_shape, in_specs=[SMEM] * len(scalars...]
    all_to_all x2, waiting for transfers between devices: 19.8 us -> 15.2 us  [exchange(): lax.all_to_all(blocks.reshape(sites, 4 * rank, width), plane, split_axis=...]
    ppermute x2 -> x1, waiting for transfers between devices: 0.01 us -> 4.37 us  [per_device(): far = lax.ppermute(here, 'y', [(i, (i + 2) % ys) for i in range(ys)])]
    ppermute x1, starting transfers between devices: 0.5 us -> 4.83 us  [per_device(): dy_h = lax.ppermute(dy, 'xh', swap)]
    reduce_scatter x1, waiting for transfers between devices: 7.74 us -> 11.2 us  [per_device(): sums = lax.psum_scatter(parts, 'z', scatter_dimension=0)]
    ppermute x4, starting transfers between devices: 8.91 us -> 5.76 us  [per_device(): weights = mine + [lax.ppermute(w, 'c', swap) for w in mine]]
    select_n x2 -> x0, other arithmetic: 2.46 us -> none  [the longest x1 1.27 us: per_device(): jnp.where(same, dy_d, dy_x)]
  transfers between devices with their start and end apart: 26 -> 25, of which waited for: 8 -> 7; matrix products, arithmetic and copies ran while one was open for 9% -> 7% of each run, Pallas kernels for 13% -> 17%
where the time goes in v3:
time: 187 us; the launch traced here: 186 us
  starting transfers between devices  58.4 us (31%)
  waiting for transfers between devices  49.1 us (26%)
  Pallas kernels  31.5 us (17%)
  between operations  14.4 us (8%)
  other arithmetic  11.6 us (6%)
  local copies, waits for them, and re-layouts  11 us (6%)
  blocking collectives  10.3 us (6%)
    pallas_call x6, Pallas kernels, call(): pl.pallas_call(kernel, out_shape=out_shape, in_specs=[SMEM] * len(scalars...  23.4 us
    all_to_all x2, starting transfers between devices, trade(): lax.all_to_all(blocks, TENSOR, split_axis=0, concat_axis=0, tiled=True)  19.1 us
    all_to_all x2, waiting for transfers between devices, exchange(): lax.all_to_all(blocks.reshape(sites, 4 * rank, width), plane, split_axis=...  15.2 us
    all_to_all x2, starting transfers between devices, exchange(): lax.all_to_all(blocks.reshape(sites, 4 * rank, width), plane, split_axis=...  12.4 us
    reduce_scatter x1, waiting for transfers between devices, per_device(): sums = lax.psum_scatter(parts, 'z', scatter_dimension=0)  11.2 us
    all_to_all x1, blocking collectives, per_device(): lax.all_to_all(asked.reshape(sites, 2, 1), plane, split_axis=0, concat_ax...  10.3 us
    all_to_all x2, waiting for transfers between devices, trade(): lax.all_to_all(blocks, TENSOR, split_axis=0, concat_axis=0, tiled=True)  8.65 us
    ppermute x1, waiting for transfers between devices, per_device(): lax.ppermute(give, ('xl', 'xh'), [(place[0], place[1]), (place[1], place[...  6.76 us
  transfers between devices with their start and end apart: 25, of which 7 were waited for; matrix products, arithmetic and copies ran while one was open for 7% of the time, Pallas kernels for 17%

profile of v3, /device:TPU:1, one launch (start us, length us, event | category | flops | bytes accessed | tf_op | source)
XLA Modules:
  0.0 186.4 jit_solution(6708814594808601826)
XLA Ops:
  12.0 10.3 %all_to_all.25 = s32[8,2,1]{1,2,0:T(1,128)S(1)} all-to-all(s32[8,2,1]{1,2,0:T(1,128)S(1)} %bitcast.60), channel_id=1, replica_groups=mesh['xl'=2,'y'=4,'c'=2,'xh'=2,'z'=8] {'y','c'}, dimensions={0} | all-to-all | bytes 128 | tf_op jit(solution)/shard_map/all_to_all | solution.py:181
  23.5 2.9 %collective-permute-done.1.theirs_ref = bf16[4,128,512]{2,1,0:T(8,128)(2,1)S(1)} collective-permute-done((bf16[4,128,512]{2,1,0:T(8,128)(2,1)S(1)}, bf16[4,128,512]{2,1,0:T(8,128)(2,1)S(1)}, u32[]{:S(2)}, u32[]{:S(2)}) %collective-permute-start.1) | collective-permute-done | bytes 524320 | tf_op jit(solution)/shard_map/ppermute | solution.py:174
  29.4 7.4 %all-to-all-start.1 = ((bf16[8,256,512]{2,1,0:T(8,128)(2,1)}), bf16[8,256,512]{2,1,0:T(8,128)(2,1)S(1)}, u32[]{:S(2)}, u32[]{:S(2)}) async-start(bf16[8,256,512]{2,1,0:T(8,128)(2,1)} %bitcast.56), calls=%async_computation.1 | async-start | bytes 4194304 | tf_op jit(solution)/shard_map/all_to_all | solution.py:228
  40.7 6.8 %collective-permute-done.3 = bf16[256,512]{1,0:T(8,128)(2,1)S(1)} collective-permute-done((bf16[256,512]{1,0:T(8,128)(2,1)S(1)}, bf16[256,512]{1,0:T(8,128)(2,1)S(1)}, u32[]{:S(2)}, u32[]{:S(2)}) %collective-permute-start.3) | collective-permute-done | bytes 262176 | tf_op jit(solution)/shard_map/ppermute | solution.py:200
  53.6 4.8 %collective-permute-start.14 = (bf16[512,512]{1,0:T(8,128)(2,1)}, bf16[512,512]{1,0:T(8,128)(2,1)}, u32[]{:S(2)}, u32[]{:S(2)}) collective-permute-start(bf16[512,512]{1,0:T(8,128)(2,1)} %broadcast_select_fusion.dy_ref.refs_0_), channel_id=1, source_target_pairs={{0,8},{8,0},{1,9},{9,1},{2,10},{10,2},{3,11},{11,3},{4,12},{12,4},... | collective-permute-start | bytes 1572872 | tf_op jit(solution)/shard_map/ppermute | solution.py:215
  58.5 4.8 %all-to-all-done.1 = bf16[8,256,512]{2,1,0:T(8,128)(2,1)S(1)} async-done(((bf16[8,256,512]{2,1,0:T(8,128)(2,1)}), bf16[8,256,512]{2,1,0:T(8,128)(2,1)S(1)}, u32[]{:S(2)}, u32[]{:S(2)}) %all-to-all-start.1) | async-done | bytes 2097184 | tf_op jit(solution)/shard_map/all_to_all | solution.py:228
  63.3 2.6 %shard_map.171 = bf16[512,128]{1,0:T(8,128)(2,1)} custom-call(s32[4]{0:T(128)S(1)} %fusion.2.owner_ref, bf16[512,512]{1,0:T(8,128)(2,1)S(1)} %copy-done.4, bf16[512,512]{1,0:T(8,128)(2,1)} %broadcast_select_fusion.dy_ref.refs_0_, bf16[16,128,512]{2,1,0:T(8,128)(2,1)S(1)} %bitcast.52), custom_call_target="tpu_custom_call" | custom-call | flops 134217728 | bytes 3145728 | tf_op jit(solution)/shard_map/pallas_call | solution.py:34
  65.9 10.6 %all-to-all-start.2 = ((bf16[16,32,128]{2,1,0:T(8,128)(2,1)}), bf16[16,32,128]{2,1,0:T(8,128)(2,1)S(1)}, u32[]{:S(2)}, u32[]{:S(2)}) async-start(bf16[16,32,128]{2,1,0:T(8,128)(2,1)} %bitcast.17), calls=%async_computation.2 | async-start | bytes 262144 | tf_op jit(solution)/shard_map/all_to_all | solution.py:257
  76.5 2.8 %collective-permute-start.16 = (bf16[512,512]{1,0:T(8,128)(2,1)}, bf16[512,512]{1,0:T(8,128)(2,1)}, u32[]{:S(2)}, u32[]{:S(2)}) collective-permute-start(bf16[512,512]{1,0:T(8,128)(2,1)} %broadcast_select_fusion.dy_ref.refs_0_), channel_id=1, source_target_pairs={{0,136},{8,128},{128,8},{136,0},{1,137},{9,129},{129,9},{137,1},{2... | collective-permute-start | bytes 1572872 | tf_op jit(solution)/shard_map/ppermute | solution.py:216
  81.4 4.4 %collective-permute-done.6.refs_3_.refs_7_ = bf16[2,256,512]{2,1,0:T(8,128)(2,1)} collective-permute-done((bf16[2,256,512]{2,1,0:T(8,128)(2,1)S(1)}, bf16[2,256,512]{2,1,0:T(8,128)(2,1)}, u32[]{:S(2)}, u32[]{:S(2)}) %collective-permute-start.6) | collective-permute-done | bytes 524320 | tf_op jit(solution)/shard_map/ppermute | solution.py:243
  86.6 2.7 %collective-permute-start.9 = (bf16[2,256,512]{2,1,0:T(8,128)(2,1)}, bf16[2,256,512]{2,1,0:T(8,128)(2,1)}, u32[]{:S(2)}, u32[]{:S(2)}) collective-permute-start(bf16[2,256,512]{2,1,0:T(8,128)(2,1)} %collective-permute-done.5.refs_2_.refs_6_), channel_id=1, source_target_pairs={{0,16},{16,0},{1,17},{17,1},{2,18},{18,2},{3,19},{19,3},{4,20},{20... | collective-permute-start | bytes 1572872 | tf_op jit(solution)/shard_map/ppermute | solution.py:263
  90.1 8.5 %all-to-all-start.3 = ((bf16[16,32,128]{2,1,0:T(8,128)(2,1)}), bf16[16,32,128]{2,1,0:T(8,128)(2,1)S(1)}, u32[]{:S(2)}, u32[]{:S(2)}) async-start(bf16[16,32,128]{2,1,0:T(8,128)(2,1)} %broadcast_in_dim.42), calls=%async_computation.3 | async-start | bytes 262144 | tf_op jit(solution)/shard_map/all_to_all | solution.py:257
  99.0 8.6 %all-to-all-done.3 = bf16[16,32,128]{2,1,0:T(8,128)(2,1)S(1)} async-done(((bf16[16,32,128]{2,1,0:T(8,128)(2,1)}), bf16[16,32,128]{2,1,0:T(8,128)(2,1)S(1)}, u32[]{:S(2)}, u32[]{:S(2)}) %all-to-all-start.3) | async-done | bytes 131104 | tf_op jit(solution)/shard_map/all_to_all | solution.py:257
  107.7 7.2 %shard_map.175 = bf16[8,2,512,256]{3,2,1,0:T(8,128)(2,1)S(1)} custom-call(s32[9]{0:T(128)S(1)} %stack.57.at_ref, bf16[512,512]{1,0:T(8,128)(2,1)} %broadcast_select_fusion.dy_ref.refs_0_, bf16[512,512]{1,0:T(8,128)(2,1)} %collective-permute-done.14.refs_1_, bf16[512,512]{1,0:T(8,128)(2,1)} %collective-permute-done.15.refs_2_, ...), custom_call_target="tpu_custom_call" | custom-call | flops 4294967296 | bytes 13631488 | tf_op jit(solution)/shard_map/pallas_call | solution.py:34
  117.0 4.4 %shard_map.172 = (bf16[16,128,512]{2,1,0:T(8,128)(2,1)}, bf16[512,512]{1,0:T(8,128)(2,1)}, bf16[512,512]{1,0:T(8,128)(2,1)}) custom-call(s32[4]{0:T(128)} %copy-done.11, bf16[512,128]{1,0:T(8,128)(2,1)} %bitcast.58, bf16[512,512]{1,0:T(8,128)(2,1)} %x_ref.3, bf16[512,512]{1,0:T(8,128)(2,1)} %broadcast_select_fusion.dy_ref.refs_0_, bf16[16,128,512]{2,1,0:T(8,128)(2,1)} %bitcast.53), custom_call_target="tpu_custom_call" | custom-call | flops 268435456 | bytes 6291456 | tf_op jit(solution)/shard_map/pallas_call | solution.py:34
  121.4 5.0 %all-to-all-start.4 = ((bf16[8,256,512]{2,1,0:T(8,128)(2,1)}), bf16[8,256,512]{2,1,0:T(8,128)(2,1)S(1)}, u32[]{:S(2)}, u32[]{:S(2)}) async-start(bf16[8,256,512]{2,1,0:T(8,128)(2,1)} %bitcast.57), calls=%async_computation.5 | async-start | bytes 4194304 | tf_op jit(solution)/shard_map/all_to_all | solution.py:228
  126.5 2.2 %copy-done.2 = bf16[16,512,256]{2,1,0:T(8,128)(2,1)S(1)} copy-done((bf16[16,512,256]{2,1,0:T(8,128)(2,1)S(1)}, bf16[16,512,256]{2,1,0:T(8,128)(2,1)}, u32[]{:S(2)}) %copy-start.2) | copy-done | bytes 4194328
  128.7 4.2 %shard_map.173 = (bf16[512,512]{1,0:T(8,128)(2,1)S(1)}, bf16[512,512]{1,0:T(8,128)(2,1)S(1)}) custom-call(s32[9]{0:T(128)S(1)} %stack.57.at_ref, bf16[8,2,512,256]{3,2,1,0:T(8,128)(2,1)S(1)} %bitcast.54, bf16[2,256,512]{2,1,0:T(8,128)(2,1)S(1)} %pad_maximum_fusion.2.refs_0_.refs_4_, bf16[2,256,512]{2,1,0:T(8,128)(2,1)} %collective-permute-done.4.refs_1_.refs_5_, ...), custom_call_target="tpu_custom_call" | custom-call | flops 2147483648 | bytes 8388608 | tf_op jit(solution)/shard_map/pallas_call | solution.py:34
  135.5 4.2 %shard_map.174 = (bf16[512,512]{1,0:T(8,128)(2,1)S(1)}, bf16[512,512]{1,0:T(8,128)(2,1)S(1)}) custom-call(s32[9]{0:T(128)S(1)} %stack.57.at_ref, bf16[8,2,512,256]{3,2,1,0:T(8,128)(2,1)S(1)} %bitcast.55, bf16[2,256,512]{2,1,0:T(8,128)(2,1)S(1)} %pad_maximum_fusion.2.refs_0_.refs_4_, bf16[2,256,512]{2,1,0:T(8,128)(2,1)} %collective-permute-done.4.refs_1_.refs_5_, ...), custom_call_target="tpu_custom_call" | custom-call | flops 2147483648 | bytes 8388608 | tf_op jit(solution)/shard_map/pallas_call | solution.py:34
  142.5 10.3 %all-to-all-done.4 = bf16[8,256,512]{2,1,0:T(8,128)(2,1)S(1)} async-done(((bf16[8,256,512]{2,1,0:T(8,128)(2,1)}), bf16[8,256,512]{2,1,0:T(8,128)(2,1)S(1)}, u32[]{:S(2)}, u32[]{:S(2)}) %all-to-all-start.4) | async-done | bytes 2097184 | tf_op jit(solution)/shard_map/all_to_all | solution.py:228
  152.8 2.6 %shard_map.176 = bf16[4,128,512]{2,1,0:T(8,128)(2,1)} custom-call(s32[16]{0:T(128)S(1)} %reshape.78.slot_ref, bf16[16,128,512]{2,1,0:T(8,128)(2,1)S(1)} %bitcast.50), custom_call_target="tpu_custom_call" | custom-call | flops 524288 | bytes 3145728 | tf_op jit(solution)/shard_map/pallas_call | solution.py:341
  155.8 11.2 %reduce-scatter.2.cloned.1.call-done = bf16[1,2,512,256]{3,2,1,0:T(8,128)(2,1)} async-done(((bf16[8,2,512,256]{3,2,1,0:T(8,128)(2,1)}), bf16[1,2,512,256]{3,2,1,0:T(8,128)(2,1)}) %reduce-scatter.2.cloned.1.call-update) | async-done | bytes 524304 | tf_op jit(solution)/shard_map/reduce_scatter | solution.py:285
  169.3 2.8 %add_convert_fusion.1 = bf16[512,512]{1,0:T(8,128)(2,1)} fusion(bf16[512,512]{1,0:T(8,128)(2,1)} %get-tuple-element.53, bf16[512,512]{1,0:T(8,128)(2,1)} %collective-permute-done.13, bf16[512,512]{1,0:T(8,128)(2,1)} %collective-permute-done.12, bf16[512,512]{1,0:T(8,128)(2,1)} %collective-permute-done.11, bf16[512,512]{1,0:T(8,128)(2,1)S(1)} %copy-done.7, ...), kind=kLoop, calls=%fused_computation.1 | loop fusion | flops 2883584 | bytes 3670017 | tf_op jit(solution)/shard_map/convert_element_type | solution.py:366
  172.1 5.5 %shard_map.177 = (f32[4,64,512]{2,1,0:T(8,128)}, f32[4,64,512]{2,1,0:T(8,128)}, f32[4,64,512]{2,1,0:T(8,128)}, f32[4,64,512]{2,1,0:T(8,128)}, f32[4,64,512]{2,1,0:T(8,128)}, /*index=5*/f32[4,64,512]{2,1,0:T(8,128)}) custom-call(s32[16]{0:T(128)} %copy-done.10, bf16[16,128,512]{2,1,0:T(8,128)(2,1)} %bitcast.51, ...), custom_call_target="tpu_custom_call" | custom-call | flops 7864320 | bytes 8388608 | tf_op jit(solution)/shard_map/pallas_call | solution.py:353
  (100 shorter events, 35.0 us)
Async XLA Ops:
  7.2 114.2 %all-gather.3.cloned.1.call-start = ((), (), s32[]{:S(2)}) async-start(), calls=%async_computation.7 | async-start | bytes 4718592 | tf_op jit(solution)/shard_map/all_gather | solution.py:194
  8.4 15.2 %collective-permute-start = (bf16[512,256]{1,0:T(8,128)(2,1)S(1)}, bf16[512,256]{1,0:T(8,128)(2,1)S(1)}, u32[]{:S(2)}, u32[]{:S(2)}) collective-permute-start(bf16[512,256]{1,0:T(8,128)(2,1)S(1)} %get-tuple-element.71), channel_id=1, source_target_pairs={{0,128},{128,0},{1,129},{129,1},{2,130},{130,2},{3,131},{131,3},{4... | collective-permute-start | bytes 786440 | tf_op jit(solution)/shard_map/ppermute | solution.py:189
  11.7 14.8 %collective-permute-start.1 = (bf16[4,128,512]{2,1,0:T(8,128)(2,1)S(1)}, bf16[4,128,512]{2,1,0:T(8,128)(2,1)S(1)}, u32[]{:S(2)}, u32[]{:S(2)}) collective-permute-start(bf16[4,128,512]{2,1,0:T(8,128)(2,1)S(1)} %pad_maximum_fusion.mine_ref), channel_id=1, source_target_pairs={{0,128},{128,0},{1,129},{129,1},{2,130},{130,2},{3,131},{131,3},{4... | collective-permute-start | bytes 1572872 | tf_op jit(solution)/shard_map/ppermute | solution.py:174
  29.4 33.9 %all-to-all-start.1 = ((bf16[8,256,512]{2,1,0:T(8,128)(2,1)}), bf16[8,256,512]{2,1,0:T(8,128)(2,1)S(1)}, u32[]{:S(2)}, u32[]{:S(2)}) async-start(bf16[8,256,512]{2,1,0:T(8,128)(2,1)} %bitcast.56), calls=%async_computation.1 | async-start | bytes 4194304 | tf_op jit(solution)/shard_map/all_to_all | solution.py:228
  37.9 9.5 %collective-permute-start.3 = (bf16[256,512]{1,0:T(8,128)(2,1)S(1)}, bf16[256,512]{1,0:T(8,128)(2,1)S(1)}, u32[]{:S(2)}, u32[]{:S(2)}) collective-permute-start(bf16[256,512]{1,0:T(8,128)(2,1)S(1)} %get-tuple-element.69), channel_id=1, source_target_pairs={{0,128},{128,136},{136,8},{8,0},{1,129},{129,137},{137,9},{9,1},{2... | collective-permute-start | bytes 786440 | tf_op jit(solution)/shard_map/ppermute | solution.py:200
  47.6 28.9 %collective-permute-start.4 = (bf16[2,256,512]{2,1,0:T(8,128)(2,1)S(1)}, bf16[2,256,512]{2,1,0:T(8,128)(2,1)}, u32[]{:S(2)}, u32[]{:S(2)}) collective-permute-start(bf16[2,256,512]{2,1,0:T(8,128)(2,1)S(1)} %pad_maximum_fusion.2.refs_0_.refs_4_), channel_id=1, source_target_pairs={{0,32},{32,64},{64,96},{96,0},{1,33},{33,65},{65,97},{97,1},{2,34}... | collective-permute-start | bytes 1572872 | tf_op jit(solution)/shard_map/ppermute | solution.py:241
  48.6 30.7 %collective-permute-start.5 = (bf16[2,256,512]{2,1,0:T(8,128)(2,1)S(1)}, bf16[2,256,512]{2,1,0:T(8,128)(2,1)}, u32[]{:S(2)}, u32[]{:S(2)}) collective-permute-start(bf16[2,256,512]{2,1,0:T(8,128)(2,1)S(1)} %pad_maximum_fusion.2.refs_0_.refs_4_), channel_id=1, source_target_pairs={{0,96},{32,0},{64,32},{96,64},{1,97},{33,1},{65,33},{97,65},{2,98}... | collective-permute-start | bytes 1572872 | tf_op jit(solution)/shard_map/ppermute | solution.py:242
  50.3 35.4 %collective-permute-start.6 = (bf16[2,256,512]{2,1,0:T(8,128)(2,1)S(1)}, bf16[2,256,512]{2,1,0:T(8,128)(2,1)}, u32[]{:S(2)}, u32[]{:S(2)}) collective-permute-start(bf16[2,256,512]{2,1,0:T(8,128)(2,1)S(1)} %pad_maximum_fusion.2.refs_0_.refs_4_), channel_id=1, source_target_pairs={{0,64},{32,96},{64,0},{96,32},{1,65},{33,97},{65,1},{97,33},{2,66}... | collective-permute-start | bytes 1572872 | tf_op jit(solution)/shard_map/ppermute | solution.py:243
  53.6 33.0 %collective-permute-start.14 = (bf16[512,512]{1,0:T(8,128)(2,1)}, bf16[512,512]{1,0:T(8,128)(2,1)}, u32[]{:S(2)}, u32[]{:S(2)}) collective-permute-start(bf16[512,512]{1,0:T(8,128)(2,1)} %broadcast_select_fusion.dy_ref.refs_0_), channel_id=1, source_target_pairs={{0,8},{8,0},{1,9},{9,1},{2,10},{10,2},{3,11},{11,3},{4,12},{12,4},... | collective-permute-start | bytes 1572872 | tf_op jit(solution)/shard_map/ppermute | solution.py:215
  58.4 30.9 %collective-permute-start.15 = (bf16[512,512]{1,0:T(8,128)(2,1)}, bf16[512,512]{1,0:T(8,128)(2,1)}, u32[]{:S(2)}, u32[]{:S(2)}) collective-permute-start(bf16[512,512]{1,0:T(8,128)(2,1)} %broadcast_select_fusion.dy_ref.refs_0_), channel_id=1, source_target_pairs={{0,128},{128,0},{1,129},{129,1},{2,130},{130,2},{3,131},{131,3},{4... | collective-permute-start | bytes 1572872 | tf_op jit(solution)/shard_map/ppermute | solution.py:214
  65.9 20.8 %all-to-all-start.2 = ((bf16[16,32,128]{2,1,0:T(8,128)(2,1)}), bf16[16,32,128]{2,1,0:T(8,128)(2,1)S(1)}, u32[]{:S(2)}, u32[]{:S(2)}) async-start(bf16[16,32,128]{2,1,0:T(8,128)(2,1)} %bitcast.17), calls=%async_computation.2 | async-start | bytes 262144 | tf_op jit(solution)/shard_map/all_to_all | solution.py:257
  76.5 31.2 %collective-permute-start.16 = (bf16[512,512]{1,0:T(8,128)(2,1)}, bf16[512,512]{1,0:T(8,128)(2,1)}, u32[]{:S(2)}, u32[]{:S(2)}) collective-permute-start(bf16[512,512]{1,0:T(8,128)(2,1)} %broadcast_select_fusion.dy_ref.refs_0_), channel_id=1, source_target_pairs={{0,136},{8,128},{128,8},{136,0},{1,137},{9,129},{129,9},{137,1},{2... | collective-permute-start | bytes 1572872 | tf_op jit(solution)/shard_map/ppermute | solution.py:216
  79.3 28.4 %collective-permute-start.7 = (bf16[2,256,512]{2,1,0:T(8,128)(2,1)S(1)}, bf16[2,256,512]{2,1,0:T(8,128)(2,1)S(1)}, u32[]{:S(2)}, u32[]{:S(2)}) collective-permute-start(bf16[2,256,512]{2,1,0:T(8,128)(2,1)S(1)} %pad_maximum_fusion.2.refs_0_.refs_4_), channel_id=1, source_target_pairs={{0,16},{16,0},{1,17},{17,1},{2,18},{18,2},{3,19},{19,3},{4,20},{20... | collective-permute-start | bytes 1572872 | tf_op jit(solution)/shard_map/ppermute | solution.py:263
  85.8 21.9 %collective-permute-start.8 = (bf16[2,256,512]{2,1,0:T(8,128)(2,1)}, bf16[2,256,512]{2,1,0:T(8,128)(2,1)}, u32[]{:S(2)}, u32[]{:S(2)}) collective-permute-start(bf16[2,256,512]{2,1,0:T(8,128)(2,1)} %collective-permute-done.4.refs_1_.refs_5_), channel_id=1, source_target_pairs={{0,16},{16,0},{1,17},{17,1},{2,18},{18,2},{3,19},{19,3},{4,20},{20... | collective-permute-start | bytes 1572872 | tf_op jit(solution)/shard_map/ppermute | solution.py:263
  86.6 21.1 %collective-permute-start.9 = (bf16[2,256,512]{2,1,0:T(8,128)(2,1)}, bf16[2,256,512]{2,1,0:T(8,128)(2,1)}, u32[]{:S(2)}, u32[]{:S(2)}) collective-permute-start(bf16[2,256,512]{2,1,0:T(8,128)(2,1)} %collective-permute-done.5.refs_2_.refs_6_), channel_id=1, source_target_pairs={{0,16},{16,0},{1,17},{17,1},{2,18},{18,2},{3,19},{19,3},{4,20},{20... | collective-permute-start | bytes 1572872 | tf_op jit(solution)/shard_map/ppermute | solution.py:263
  89.4 18.3 %collective-permute-start.10 = (bf16[2,256,512]{2,1,0:T(8,128)(2,1)}, bf16[2,256,512]{2,1,0:T(8,128)(2,1)}, u32[]{:S(2)}, u32[]{:S(2)}) collective-permute-start(bf16[2,256,512]{2,1,0:T(8,128)(2,1)} %collective-permute-done.6.refs_3_.refs_7_), channel_id=1, source_target_pairs={{0,16},{16,0},{1,17},{17,1},{2,18},{18,2},{3,19},{19,3},{4,20},{20... | collective-permute-start | bytes 1572872 | tf_op jit(solution)/shard_map/ppermute | solution.py:263
  90.1 17.5 %all-to-all-start.3 = ((bf16[16,32,128]{2,1,0:T(8,128)(2,1)}), bf16[16,32,128]{2,1,0:T(8,128)(2,1)S(1)}, u32[]{:S(2)}, u32[]{:S(2)}) async-start(bf16[16,32,128]{2,1,0:T(8,128)(2,1)} %broadcast_in_dim.42), calls=%async_computation.3 | async-start | bytes 262144 | tf_op jit(solution)/shard_map/all_to_all | solution.py:257
  98.6 68.4 %reduce-scatter.2.cloned.1.call-start = ((), (), s32[]{:S(2)}) async-start(), calls=%async_computation.6 | async-start | bytes 4718592 | tf_op jit(solution)/shard_map/reduce_scatter | solution.py:285
  121.4 31.4 %all-to-all-start.4 = ((bf16[8,256,512]{2,1,0:T(8,128)(2,1)}), bf16[8,256,512]{2,1,0:T(8,128)(2,1)S(1)}, u32[]{:S(2)}, u32[]{:S(2)}) async-start(bf16[8,256,512]{2,1,0:T(8,128)(2,1)} %bitcast.57), calls=%async_computation.5 | async-start | bytes 4194304 | tf_op jit(solution)/shard_map/all_to_all | solution.py:228
  134.5 34.7 %collective-permute-start.13 = (bf16[512,512]{1,0:T(8,128)(2,1)}, bf16[512,512]{1,0:T(8,128)(2,1)}, u32[]{:S(2)}, u32[]{:S(2)}) collective-permute-start(bf16[512,512]{1,0:T(8,128)(2,1)} %broadcast_select_fusion.1), channel_id=1, source_target_pairs={{0,8},{8,0},{1,9},{9,1},{2,10},{10,2},{3,11},{11,3},{4,12},{12,4},... | collective-permute-start | bytes 1572872 | tf_op jit(solution)/shard_map/ppermute | solution.py:323
  140.8 28.4 %collective-permute-start.12 = (bf16[512,512]{1,0:T(8,128)(2,1)}, bf16[512,512]{1,0:T(8,128)(2,1)}, u32[]{:S(2)}, u32[]{:S(2)}) collective-permute-start(bf16[512,512]{1,0:T(8,128)(2,1)} %get-tuple-element.63), channel_id=1, source_target_pairs={{0,136},{8,128},{128,8},{136,0},{1,137},{9,129},{129,9},{137,1},{2... | collective-permute-start | bytes 1572872 | tf_op jit(solution)/shard_map/ppermute | solution.py:322
  142.5 26.8 %collective-permute-start.11 = (bf16[512,512]{1,0:T(8,128)(2,1)}, bf16[512,512]{1,0:T(8,128)(2,1)}, u32[]{:S(2)}, u32[]{:S(2)}) collective-permute-start(bf16[512,512]{1,0:T(8,128)(2,1)} %get-tuple-element.62), channel_id=1, source_target_pairs={{0,128},{128,0},{1,129},{129,1},{2,130},{130,2},{3,131},{131,3},{4... | collective-permute-start | bytes 1572872 | tf_op jit(solution)/shard_map/ppermute | solution.py:321
  155.4 16.6 %collective-permute-start.18 = (bf16[4,128,512]{2,1,0:T(8,128)(2,1)}, bf16[4,128,512]{2,1,0:T(8,128)(2,1)}, u32[]{:S(2)}, u32[]{:S(2)}) collective-permute-start(bf16[4,128,512]{2,1,0:T(8,128)(2,1)} %shard_map.176), channel_id=1, source_target_pairs={{0,128},{128,0},{1,129},{129,1},{2,130},{130,2},{3,131},{131,3},{4... | collective-permute-start | bytes 1572872 | tf_op jit(solution)/shard_map/ppermute | solution.py:364
  168.0 9.6 %collective-permute-start.17 = (bf16[512,256]{1,0:T(8,128)(2,1)S(1)}, bf16[512,256]{1,0:T(8,128)(2,1)}, u32[]{:S(2)}, u32[]{:S(2)}) collective-permute-start(bf16[512,256]{1,0:T(8,128)(2,1)S(1)} %slice_bitcast_fusion), channel_id=1, source_target_pairs={{0,128},{128,0},{1,129},{129,1},{2,130},{130,2},{3,131},{131,3},{4... | collective-permute-start | bytes 786440 | tf_op jit(solution)/shard_map/ppermute | solution.py:287
  (19 other events, 369.1 us)
Sparse Core Ops, SparseCore 0:
  27.4 62.6 all-gather.2
  117.1 49.8 reduce-scatter.1

commit v4 on v3

--- a/solution.py
+++ b/solution.py
@@ -271,7 +271,6 @@
     low_share = jnp.sum(terms.astype(f32), axis=0).astype(bf16)
     low = trade(jnp.broadcast_to(low_share[None], (peers, share, 2 * rank)))
     low = low.reshape(tok_rows, 2 * rank)
-    at, low = lax.optimization_barrier((at, low))
     big = 2 * tok_rows * planes * width * half
     same = xh == 0
     parts = call(
@@ -282,6 +281,7 @@
         4 * big,
         13 * 2**20,
     )
+    parts, low = lax.optimization_barrier((parts, low))
     sums = lax.psum_scatter(parts, "z", scatter_dimension=0)
     sum_own, sum_got = sums[0], sums[1]
     sum_back = lax.ppermute(sum_got, "xl", swap)
@@ -306,8 +306,8 @@
     x_all, grads_sent, lora_out = lax.optimization_barrier((x_all, grads_sent, lora_out))
     grad_parts = exchange(grads_sent)
     block = jax.ShapeDtypeStruct((tok_rows, width), bf16)
-    forward = [
-        call(
+    def forward(row, at):
+        return call(
             functools.partial(forward_kernel, row=row),
             (block, block),
             [x_all, *weights],
@@ -315,9 +315,10 @@
             2 * big,
             8 * 2**20,
         )
-        for row in (1, 0)
-    ]
-    (got_a, got_b), (own_a, own_b) = forward
+
+    got_a, got_b = forward(1, at)
+    at, got_a, got_b = lax.optimization_barrier((at, got_a, got_b))
+    own_a, own_b = forward(0, at)
     from_x = lax.ppermute(jnp.where(same, got_a, got_b), "xl", swap)
     from_d = lax.ppermute(jnp.where(same, got_b, got_a), ("xl", "xh"), cross)
     from_h = lax.ppermute(jnp.where(same, own_b, own_a), "xh", swap)

time: 187 us -> 187 us (level)
    all_to_all x2, waiting for transfers between devices: 8.65 us -> 0.01 us  [trade(): lax.all_to_all(blocks, TENSOR, split_axis=0, concat_axis=0, tiled=True)]
    ppermute x1, waiting for transfers between devices: 0.01 us -> 7.75 us  [per_device(): above = lax.ppermute(here, 'y', down_ring)]
    reduce_scatter x1, waiting for transfers between devices: 11.2 us -> 16.9 us  [per_device(): sums = lax.psum_scatter(parts, 'z', scatter_dimension=0)]
    ppermute x1, waiting for transfers between devices: 4.37 us -> 0.01 us  [per_device(): far = lax.ppermute(here, 'y', [(i, (i + 2) % ys) for i in range(ys)])]
    ppermute x4, starting transfers between devices: 5.76 us -> 2.45 us  [per_device(): weights = mine + [lax.ppermute(w, 'c', swap) for w in mine]]
    all_to_all x2, starting transfers between devices: 12.4 us -> 15.3 us  [exchange(): lax.all_to_all(blocks.reshape(sites, 4 * rank, width), plane, split_axis=...]
    ppermute x1, starting transfers between devices: 4.83 us -> 2.75 us  [per_device(): dy_h = lax.ppermute(dy, 'xh', swap)]
    ppermute x1, starting transfers between devices: 0.01 us -> 2.03 us  [per_device(): dy_x = lax.ppermute(dy, 'xl', swap)]
  transfers between devices with their start and end apart: 25 -> 25, of which waited for: 7 -> 6; matrix products, arithmetic and copies ran while one was open for 7% -> 7% of each run, Pallas kernels for 17% -> 17%
where the time goes in v4:
time: 187 us
  starting transfers between devices  58.2 us (31%)
  waiting for transfers between devices  49.5 us (26%)
  Pallas kernels  31.5 us (17%)
  between operations  14.3 us (8%)
  other arithmetic  11.7 us (6%)
  local copies, waits for them, and re-layouts  11.1 us (6%)
  blocking collectives  10.3 us (6%)
    pallas_call x6, Pallas kernels, call(): pl.pallas_call(kernel, out_shape=out_shape, in_specs=[SMEM] * len(scalars...  23.4 us
    all_to_all x2, starting transfers between devices, trade(): lax.all_to_all(blocks, TENSOR, split_axis=0, concat_axis=0, tiled=True)  19 us
    reduce_scatter x1, waiting for transfers between devices, per_device(): sums = lax.psum_scatter(parts, 'z', scatter_dimension=0)  16.9 us
    all_to_all x2, starting transfers between devices, exchange(): lax.all_to_all(blocks.reshape(sites, 4 * rank, width), plane, split_axis=...  15.3 us
    all_to_all x2, waiting for transfers between devices, exchange(): lax.all_to_all(blocks.reshape(sites, 4 * rank, width), plane, split_axis=...  15.1 us
    all_to_all x1, blocking collectives, per_device(): lax.all_to_all(asked.reshape(sites, 2, 1), plane, split_axis=0, concat_ax...  10.3 us
    ppermute x1, waiting for transfers between devices, per_device(): above = lax.ppermute(here, 'y', down_ring)  7.75 us
    ppermute x1, waiting for transfers between devices, per_device(): lax.ppermute(give, ('xl', 'xh'), [(place[0], place[1]), (place[1], place[...  6.76 us
  transfers between devices with their start and end apart: 25, of which 6 were waited for; matrix products, arithmetic and copies ran while one was open for 7% of the time, Pallas kernels for 17%

profile of v4, /device:TPU:1, one launch (start us, length us, event | category | flops | bytes accessed | tf_op | source)
XLA Modules:
  0.0 186.6 jit_solution(3729596587558450760)
XLA Ops:
  12.0 10.3 %all_to_all.25 = s32[8,2,1]{1,2,0:T(1,128)S(1)} all-to-all(s32[8,2,1]{1,2,0:T(1,128)S(1)} %bitcast.60), channel_id=1, replica_groups=mesh['xl'=2,'y'=4,'c'=2,'xh'=2,'z'=8] {'y','c'}, dimensions={0} | all-to-all | bytes 128 | tf_op jit(solution)/shard_map/all_to_all | solution.py:181
  23.5 2.9 %collective-permute-done.1.theirs_ref = bf16[4,128,512]{2,1,0:T(8,128)(2,1)S(1)} collective-permute-done((bf16[4,128,512]{2,1,0:T(8,128)(2,1)S(1)}, bf16[4,128,512]{2,1,0:T(8,128)(2,1)S(1)}, u32[]{:S(2)}, u32[]{:S(2)}) %collective-permute-start.1) | collective-permute-done | bytes 524320 | tf_op jit(solution)/shard_map/ppermute | solution.py:174
  29.4 7.4 %all-to-all-start.1 = ((bf16[8,256,512]{2,1,0:T(8,128)(2,1)}), bf16[8,256,512]{2,1,0:T(8,128)(2,1)S(1)}, u32[]{:S(2)}, u32[]{:S(2)}) async-start(bf16[8,256,512]{2,1,0:T(8,128)(2,1)} %bitcast.56), calls=%async_computation.1 | async-start | bytes 4194304 | tf_op jit(solution)/shard_map/all_to_all | solution.py:228
  40.7 6.8 %collective-permute-done.6 = bf16[256,512]{1,0:T(8,128)(2,1)S(1)} collective-permute-done((bf16[256,512]{1,0:T(8,128)(2,1)S(1)}, bf16[256,512]{1,0:T(8,128)(2,1)S(1)}, u32[]{:S(2)}, u32[]{:S(2)}) %collective-permute-start.6) | collective-permute-done | bytes 262176 | tf_op jit(solution)/shard_map/ppermute | solution.py:200
  47.6 2.6 %collective-permute-start.9 = (bf16[2,256,512]{2,1,0:T(8,128)(2,1)S(1)}, bf16[2,256,512]{2,1,0:T(8,128)(2,1)}, u32[]{:S(2)}, u32[]{:S(2)}) collective-permute-start(bf16[2,256,512]{2,1,0:T(8,128)(2,1)S(1)} %pad_maximum_fusion.2.refs_4_.refs_0_), channel_id=1, source_target_pairs={{0,64},{32,96},{64,0},{96,32},{1,65},{33,97},{65,1},{97,33},{2,66}... | collective-permute-start | bytes 1572872 | tf_op jit(solution)/shard_map/ppermute | solution.py:243
  53.6 2.5 %collective-permute-start.4 = (bf16[512,512]{1,0:T(8,128)(2,1)}, bf16[512,512]{1,0:T(8,128)(2,1)}, u32[]{:S(2)}, u32[]{:S(2)}) collective-permute-start(bf16[512,512]{1,0:T(8,128)(2,1)} %broadcast_select_fusion.dy_ref.refs_0_), channel_id=1, source_target_pairs={{0,136},{8,128},{128,8},{136,0},{1,137},{9,129},{129,9},{137,1},{2... | collective-permute-start | bytes 1572872 | tf_op jit(solution)/shard_map/ppermute | solution.py:216
  58.1 5.0 %all-to-all-done.1 = bf16[8,256,512]{2,1,0:T(8,128)(2,1)S(1)} async-done(((bf16[8,256,512]{2,1,0:T(8,128)(2,1)}), bf16[8,256,512]{2,1,0:T(8,128)(2,1)S(1)}, u32[]{:S(2)}, u32[]{:S(2)}) %all-to-all-start.1) | async-done | bytes 2097184 | tf_op jit(solution)/shard_map/all_to_all | solution.py:228
  63.2 2.5 %shard_map.171 = bf16[512,128]{1,0:T(8,128)(2,1)} custom-call(s32[4]{0:T(128)S(1)} %fusion.6.owner_ref, bf16[512,512]{1,0:T(8,128)(2,1)S(1)} %copy-done.4, bf16[512,512]{1,0:T(8,128)(2,1)} %broadcast_select_fusion.dy_ref.refs_0_, bf16[16,128,512]{2,1,0:T(8,128)(2,1)S(1)} %bitcast.52), custom_call_target="tpu_custom_call" | custom-call | flops 134217728 | bytes 3145728 | tf_op jit(solution)/shard_map/pallas_call | solution.py:34
  65.7 10.8 %all-to-all-start.2 = ((bf16[16,32,128]{2,1,0:T(8,128)(2,1)}), bf16[16,32,128]{2,1,0:T(8,128)(2,1)S(1)}, u32[]{:S(2)}, u32[]{:S(2)}) async-start(bf16[16,32,128]{2,1,0:T(8,128)(2,1)} %bitcast.22), calls=%async_computation.2 | async-start | bytes 262144 | tf_op jit(solution)/shard_map/all_to_all | solution.py:257
  76.5 7.8 %collective-permute-done.8.refs_6_.refs_2_ = bf16[2,256,512]{2,1,0:T(8,128)(2,1)} collective-permute-done((bf16[2,256,512]{2,1,0:T(8,128)(2,1)S(1)}, bf16[2,256,512]{2,1,0:T(8,128)(2,1)}, u32[]{:S(2)}, u32[]{:S(2)}) %collective-permute-start.8) | collective-permute-done | bytes 524320 | tf_op jit(solution)/shard_map/ppermute | solution.py:242
  84.2 2.7 %collective-permute-start.2 = (bf16[512,512]{1,0:T(8,128)(2,1)}, bf16[512,512]{1,0:T(8,128)(2,1)}, u32[]{:S(2)}, u32[]{:S(2)}) collective-permute-start(bf16[512,512]{1,0:T(8,128)(2,1)} %broadcast_select_fusion.dy_ref.refs_0_), channel_id=1, source_target_pairs={{0,8},{8,0},{1,9},{9,1},{2,10},{10,2},{3,11},{11,3},{4,12},{12,4},... | collective-permute-start | bytes 1572872 | tf_op jit(solution)/shard_map/ppermute | solution.py:215
  90.3 8.3 %all-to-all-start.3 = ((bf16[16,32,128]{2,1,0:T(8,128)(2,1)}), bf16[16,32,128]{2,1,0:T(8,128)(2,1)S(1)}, u32[]{:S(2)}, u32[]{:S(2)}) async-start(bf16[16,32,128]{2,1,0:T(8,128)(2,1)} %broadcast_in_dim.42), calls=%async_computation.3 | async-start | bytes 262144 | tf_op jit(solution)/shard_map/all_to_all | solution.py:257
  98.8 7.2 %shard_map.172 = bf16[8,2,512,256]{3,2,1,0:T(8,128)(2,1)S(1)} custom-call(s32[9]{0:T(128)S(1)} %stack.57.at_ref, bf16[512,512]{1,0:T(8,128)(2,1)} %broadcast_select_fusion.dy_ref.refs_0_, bf16[512,512]{1,0:T(8,128)(2,1)} %collective-permute-done.2.refs_1_, bf16[512,512]{1,0:T(8,128)(2,1)} %collective-permute-done.3.refs_2_, ...), custom_call_target="tpu_custom_call" | custom-call | flops 4294967296 | bytes 13631488 | tf_op jit(solution)/shard_map/pallas_call | solution.py:34
  108.7 4.4 %shard_map.173 = (bf16[16,128,512]{2,1,0:T(8,128)(2,1)}, bf16[512,512]{1,0:T(8,128)(2,1)}, bf16[512,512]{1,0:T(8,128)(2,1)}) custom-call(s32[4]{0:T(128)} %copy-done.11, bf16[512,128]{1,0:T(8,128)(2,1)} %bitcast.58, bf16[512,512]{1,0:T(8,128)(2,1)} %x_ref.3, bf16[512,512]{1,0:T(8,128)(2,1)} %broadcast_select_fusion.dy_ref.refs_0_, bf16[16,128,512]{2,1,0:T(8,128)(2,1)} %bitcast.53), custom_call_target="tpu_custom_call" | custom-call | flops 268435456 | bytes 6291456 | tf_op jit(solution)/shard_map/pallas_call | solution.py:34
  113.2 7.9 %all-to-all-start.4 = ((bf16[8,256,512]{2,1,0:T(8,128)(2,1)}), bf16[8,256,512]{2,1,0:T(8,128)(2,1)S(1)}, u32[]{:S(2)}, u32[]{:S(2)}) async-start(bf16[8,256,512]{2,1,0:T(8,128)(2,1)} %bitcast.57), calls=%async_computation.5 | async-start | bytes 4194304 | tf_op jit(solution)/shard_map/all_to_all | solution.py:228
  121.0 2.2 %copy-done.2 = bf16[16,512,256]{2,1,0:T(8,128)(2,1)S(1)} copy-done((bf16[16,512,256]{2,1,0:T(8,128)(2,1)S(1)}, bf16[16,512,256]{2,1,0:T(8,128)(2,1)}, u32[]{:S(2)}) %copy-start.2) | copy-done | bytes 4194328
  123.2 4.2 %shard_map.174 = (bf16[512,512]{1,0:T(8,128)(2,1)S(1)}, bf16[512,512]{1,0:T(8,128)(2,1)S(1)}) custom-call(s32[9]{0:T(128)S(1)} %stack.57.at_ref, bf16[8,2,512,256]{3,2,1,0:T(8,128)(2,1)S(1)} %bitcast.54, bf16[2,256,512]{2,1,0:T(8,128)(2,1)S(1)} %pad_maximum_fusion.2.refs_4_.refs_0_, bf16[2,256,512]{2,1,0:T(8,128)(2,1)} %collective-permute-done.7.refs_5_.refs_1_, ...), custom_call_target="tpu_custom_call" | custom-call | flops 2147483648 | bytes 8388608 | tf_op jit(solution)/shard_map/pallas_call | solution.py:34
  129.1 2.3 %collective-permute-start.15 = (bf16[512,512]{1,0:T(8,128)(2,1)}, bf16[512,512]{1,0:T(8,128)(2,1)}, u32[]{:S(2)}, u32[]{:S(2)}) collective-permute-start(bf16[512,512]{1,0:T(8,128)(2,1)} %get-tuple-element.69), channel_id=1, source_target_pairs={{0,136},{8,128},{128,8},{136,0},{1,137},{9,129},{129,9},{137,1},{2... | collective-permute-start | bytes 1572872 | tf_op jit(solution)/shard_map/ppermute | solution.py:323
  131.4 4.2 %shard_map.175 = (bf16[512,512]{1,0:T(8,128)(2,1)S(1)}, bf16[512,512]{1,0:T(8,128)(2,1)S(1)}) custom-call(s32[9]{0:T(128)S(1)} %stack.57.at_ref, bf16[8,2,512,256]{3,2,1,0:T(8,128)(2,1)S(1)} %bitcast.55, bf16[2,256,512]{2,1,0:T(8,128)(2,1)S(1)} %pad_maximum_fusion.2.refs_4_.refs_0_, bf16[2,256,512]{2,1,0:T(8,128)(2,1)} %collective-permute-done.7.refs_5_.refs_1_, ...), custom_call_target="tpu_custom_call" | custom-call | flops 2147483648 | bytes 8388608 | tf_op jit(solution)/shard_map/pallas_call | solution.py:34
  137.4 10.1 %all-to-all-done.4 = bf16[8,256,512]{2,1,0:T(8,128)(2,1)S(1)} async-done(((bf16[8,256,512]{2,1,0:T(8,128)(2,1)}), bf16[8,256,512]{2,1,0:T(8,128)(2,1)S(1)}, u32[]{:S(2)}, u32[]{:S(2)}) %all-to-all-start.4) | async-done | bytes 2097184 | tf_op jit(solution)/shard_map/all_to_all | solution.py:228
  147.5 2.6 %shard_map.176 = bf16[4,128,512]{2,1,0:T(8,128)(2,1)} custom-call(s32[16]{0:T(128)S(1)} %reshape.78.slot_ref, bf16[16,128,512]{2,1,0:T(8,128)(2,1)S(1)} %bitcast.50), custom_call_target="tpu_custom_call" | custom-call | flops 524288 | bytes 3145728 | tf_op jit(solution)/shard_map/pallas_call | solution.py:342
  150.3 16.9 %reduce-scatter.2.cloned.1.call-done = bf16[1,2,512,256]{3,2,1,0:T(8,128)(2,1)} async-done(((bf16[8,2,512,256]{3,2,1,0:T(8,128)(2,1)}), bf16[1,2,512,256]{3,2,1,0:T(8,128)(2,1)}) %reduce-scatter.2.cloned.1.call-update) | async-done | bytes 524304 | tf_op jit(solution)/shard_map/reduce_scatter | solution.py:285
  169.5 2.8 %add_convert_fusion.1 = bf16[512,512]{1,0:T(8,128)(2,1)} fusion(bf16[512,512]{1,0:T(8,128)(2,1)} %get-tuple-element.58, bf16[512,512]{1,0:T(8,128)(2,1)} %collective-permute-done.16, bf16[512,512]{1,0:T(8,128)(2,1)} %collective-permute-done.15, bf16[512,512]{1,0:T(8,128)(2,1)} %collective-permute-done.14, bf16[512,512]{1,0:T(8,128)(2,1)S(1)} %copy-done.7, ...), kind=kLoop, calls=%fused_computation.1 | loop fusion | flops 2883584 | bytes 3670017 | tf_op jit(solution)/shard_map/convert_element_type | solution.py:367
  172.3 5.5 %shard_map.177 = (f32[4,64,512]{2,1,0:T(8,128)}, f32[4,64,512]{2,1,0:T(8,128)}, f32[4,64,512]{2,1,0:T(8,128)}, f32[4,64,512]{2,1,0:T(8,128)}, f32[4,64,512]{2,1,0:T(8,128)}, /*index=5*/f32[4,64,512]{2,1,0:T(8,128)}) custom-call(s32[16]{0:T(128)} %copy-done.10, bf16[16,128,512]{2,1,0:T(8,128)(2,1)} %bitcast.51, ...), custom_call_target="tpu_custom_call" | custom-call | flops 7864320 | bytes 8388608 | tf_op jit(solution)/shard_map/pallas_call | solution.py:354
  (100 shorter events, 32.3 us)
Async XLA Ops:
  7.2 106.0 %all-gather.3.cloned.1.call-start = ((), (), s32[]{:S(2)}) async-start(), calls=%async_computation.7 | async-start | bytes 4718592 | tf_op jit(solution)/shard_map/all_gather | solution.py:194
  8.4 15.2 %collective-permute-start = (bf16[512,256]{1,0:T(8,128)(2,1)S(1)}, bf16[512,256]{1,0:T(8,128)(2,1)S(1)}, u32[]{:S(2)}, u32[]{:S(2)}) collective-permute-start(bf16[512,256]{1,0:T(8,128)(2,1)S(1)} %get-tuple-element.77), channel_id=1, source_target_pairs={{0,128},{128,0},{1,129},{129,1},{2,130},{130,2},{3,131},{131,3},{4... | collective-permute-start | bytes 786440 | tf_op jit(solution)/shard_map/ppermute | solution.py:189
  11.7 14.8 %collective-permute-start.1 = (bf16[4,128,512]{2,1,0:T(8,128)(2,1)S(1)}, bf16[4,128,512]{2,1,0:T(8,128)(2,1)S(1)}, u32[]{:S(2)}, u32[]{:S(2)}) collective-permute-start(bf16[4,128,512]{2,1,0:T(8,128)(2,1)S(1)} %pad_maximum_fusion.mine_ref), channel_id=1, source_target_pairs={{0,128},{128,0},{1,129},{129,1},{2,130},{130,2},{3,131},{131,3},{4... | collective-permute-start | bytes 1572872 | tf_op jit(solution)/shard_map/ppermute | solution.py:174
  29.4 33.8 %all-to-all-start.1 = ((bf16[8,256,512]{2,1,0:T(8,128)(2,1)}), bf16[8,256,512]{2,1,0:T(8,128)(2,1)S(1)}, u32[]{:S(2)}, u32[]{:S(2)}) async-start(bf16[8,256,512]{2,1,0:T(8,128)(2,1)} %bitcast.56), calls=%async_computation.1 | async-start | bytes 4194304 | tf_op jit(solution)/shard_map/all_to_all | solution.py:228
  37.9 9.5 %collective-permute-start.6 = (bf16[256,512]{1,0:T(8,128)(2,1)S(1)}, bf16[256,512]{1,0:T(8,128)(2,1)S(1)}, u32[]{:S(2)}, u32[]{:S(2)}) collective-permute-start(bf16[256,512]{1,0:T(8,128)(2,1)S(1)} %get-tuple-element.75), channel_id=1, source_target_pairs={{0,128},{128,136},{136,8},{8,0},{1,129},{129,137},{137,9},{9,1},{2... | collective-permute-start | bytes 786440 | tf_op jit(solution)/shard_map/ppermute | solution.py:200
  47.6 40.6 %collective-permute-start.9 = (bf16[2,256,512]{2,1,0:T(8,128)(2,1)S(1)}, bf16[2,256,512]{2,1,0:T(8,128)(2,1)}, u32[]{:S(2)}, u32[]{:S(2)}) collective-permute-start(bf16[2,256,512]{2,1,0:T(8,128)(2,1)S(1)} %pad_maximum_fusion.2.refs_4_.refs_0_), channel_id=1, source_target_pairs={{0,64},{32,96},{64,0},{96,32},{1,65},{33,97},{65,1},{97,33},{2,66}... | collective-permute-start | bytes 1572872 | tf_op jit(solution)/shard_map/ppermute | solution.py:243
  50.2 34.1 %collective-permute-start.8 = (bf16[2,256,512]{2,1,0:T(8,128)(2,1)S(1)}, bf16[2,256,512]{2,1,0:T(8,128)(2,1)}, u32[]{:S(2)}, u32[]{:S(2)}) collective-permute-start(bf16[2,256,512]{2,1,0:T(8,128)(2,1)S(1)} %pad_maximum_fusion.2.refs_4_.refs_0_), channel_id=1, source_target_pairs={{0,96},{32,0},{64,32},{96,64},{1,97},{33,1},{65,33},{97,65},{2,98}... | collective-permute-start | bytes 1572872 | tf_op jit(solution)/shard_map/ppermute | solution.py:242
  51.0 35.9 %collective-permute-start.7 = (bf16[2,256,512]{2,1,0:T(8,128)(2,1)S(1)}, bf16[2,256,512]{2,1,0:T(8,128)(2,1)}, u32[]{:S(2)}, u32[]{:S(2)}) collective-permute-start(bf16[2,256,512]{2,1,0:T(8,128)(2,1)S(1)} %pad_maximum_fusion.2.refs_4_.refs_0_), channel_id=1, source_target_pairs={{0,32},{32,64},{64,96},{96,0},{1,33},{33,65},{65,97},{97,1},{2,34}... | collective-permute-start | bytes 1572872 | tf_op jit(solution)/shard_map/ppermute | solution.py:241
  53.6 34.7 %collective-permute-start.4 = (bf16[512,512]{1,0:T(8,128)(2,1)}, bf16[512,512]{1,0:T(8,128)(2,1)}, u32[]{:S(2)}, u32[]{:S(2)}) collective-permute-start(bf16[512,512]{1,0:T(8,128)(2,1)} %broadcast_select_fusion.dy_ref.refs_0_), channel_id=1, source_target_pairs={{0,136},{8,128},{128,8},{136,0},{1,137},{9,129},{129,9},{137,1},{2... | collective-permute-start | bytes 1572872 | tf_op jit(solution)/shard_map/ppermute | solution.py:216
  56.1 33.3 %collective-permute-start.3 = (bf16[512,512]{1,0:T(8,128)(2,1)}, bf16[512,512]{1,0:T(8,128)(2,1)}, u32[]{:S(2)}, u32[]{:S(2)}) collective-permute-start(bf16[512,512]{1,0:T(8,128)(2,1)} %broadcast_select_fusion.dy_ref.refs_0_), channel_id=1, source_target_pairs={{0,128},{128,0},{1,129},{129,1},{2,130},{130,2},{3,131},{131,3},{4... | collective-permute-start | bytes 1572872 | tf_op jit(solution)/shard_map/ppermute | solution.py:214
  65.7 22.5 %all-to-all-start.2 = ((bf16[16,32,128]{2,1,0:T(8,128)(2,1)}), bf16[16,32,128]{2,1,0:T(8,128)(2,1)S(1)}, u32[]{:S(2)}, u32[]{:S(2)}) async-start(bf16[16,32,128]{2,1,0:T(8,128)(2,1)} %bitcast.22), calls=%async_computation.2 | async-start | bytes 262144 | tf_op jit(solution)/shard_map/all_to_all | solution.py:257
  84.2 14.5 %collective-permute-start.2 = (bf16[512,512]{1,0:T(8,128)(2,1)}, bf16[512,512]{1,0:T(8,128)(2,1)}, u32[]{:S(2)}, u32[]{:S(2)}) collective-permute-start(bf16[512,512]{1,0:T(8,128)(2,1)} %broadcast_select_fusion.dy_ref.refs_0_), channel_id=1, source_target_pairs={{0,8},{8,0},{1,9},{9,1},{2,10},{10,2},{3,11},{11,3},{4,12},{12,4},... | collective-permute-start | bytes 1572872 | tf_op jit(solution)/shard_map/ppermute | solution.py:215
  87.0 11.8 %collective-permute-start.10 = (bf16[2,256,512]{2,1,0:T(8,128)(2,1)S(1)}, bf16[2,256,512]{2,1,0:T(8,128)(2,1)S(1)}, u32[]{:S(2)}, u32[]{:S(2)}) collective-permute-start(bf16[2,256,512]{2,1,0:T(8,128)(2,1)S(1)} %pad_maximum_fusion.2.refs_4_.refs_0_), channel_id=1, source_target_pairs={{0,16},{16,0},{1,17},{17,1},{2,18},{18,2},{3,19},{19,3},{4,20},{20... | collective-permute-start | bytes 1572872 | tf_op jit(solution)/shard_map/ppermute | solution.py:263
  88.2 10.6 %collective-permute-start.11 = (bf16[2,256,512]{2,1,0:T(8,128)(2,1)}, bf16[2,256,512]{2,1,0:T(8,128)(2,1)}, u32[]{:S(2)}, u32[]{:S(2)}) collective-permute-start(bf16[2,256,512]{2,1,0:T(8,128)(2,1)} %collective-permute-done.7.refs_5_.refs_1_), channel_id=1, source_target_pairs={{0,16},{16,0},{1,17},{17,1},{2,18},{18,2},{3,19},{19,3},{4,20},{20... | collective-permute-start | bytes 1572872 | tf_op jit(solution)/shard_map/ppermute | solution.py:263
  88.3 10.5 %collective-permute-start.12 = (bf16[2,256,512]{2,1,0:T(8,128)(2,1)}, bf16[2,256,512]{2,1,0:T(8,128)(2,1)}, u32[]{:S(2)}, u32[]{:S(2)}) collective-permute-start(bf16[2,256,512]{2,1,0:T(8,128)(2,1)} %collective-permute-done.8.refs_6_.refs_2_), channel_id=1, source_target_pairs={{0,16},{16,0},{1,17},{17,1},{2,18},{18,2},{3,19},{19,3},{4,20},{20... | collective-permute-start | bytes 1572872 | tf_op jit(solution)/shard_map/ppermute | solution.py:263
  89.4 9.4 %collective-permute-start.13 = (bf16[2,256,512]{2,1,0:T(8,128)(2,1)}, bf16[2,256,512]{2,1,0:T(8,128)(2,1)}, u32[]{:S(2)}, u32[]{:S(2)}) collective-permute-start(bf16[2,256,512]{2,1,0:T(8,128)(2,1)} %collective-permute-done.9.refs_7_.refs_3_), channel_id=1, source_target_pairs={{0,16},{16,0},{1,17},{17,1},{2,18},{18,2},{3,19},{19,3},{4,20},{20... | collective-permute-start | bytes 1572872 | tf_op jit(solution)/shard_map/ppermute | solution.py:263
  90.3 17.8 %all-to-all-start.3 = ((bf16[16,32,128]{2,1,0:T(8,128)(2,1)}), bf16[16,32,128]{2,1,0:T(8,128)(2,1)S(1)}, u32[]{:S(2)}, u32[]{:S(2)}) async-start(bf16[16,32,128]{2,1,0:T(8,128)(2,1)} %broadcast_in_dim.42), calls=%async_computation.3 | async-start | bytes 262144 | tf_op jit(solution)/shard_map/all_to_all | solution.py:257
  98.5 68.7 %reduce-scatter.2.cloned.1.call-start = ((), (), s32[]{:S(2)}) async-start(), calls=%async_computation.6 | async-start | bytes 4718592 | tf_op jit(solution)/shard_map/reduce_scatter | solution.py:285
  113.2 34.3 %all-to-all-start.4 = ((bf16[8,256,512]{2,1,0:T(8,128)(2,1)}), bf16[8,256,512]{2,1,0:T(8,128)(2,1)S(1)}, u32[]{:S(2)}, u32[]{:S(2)}) async-start(bf16[8,256,512]{2,1,0:T(8,128)(2,1)} %bitcast.57), calls=%async_computation.5 | async-start | bytes 4194304 | tf_op jit(solution)/shard_map/all_to_all | solution.py:228
  128.5 41.0 %collective-permute-start.14 = (bf16[512,512]{1,0:T(8,128)(2,1)}, bf16[512,512]{1,0:T(8,128)(2,1)}, u32[]{:S(2)}, u32[]{:S(2)}) collective-permute-start(bf16[512,512]{1,0:T(8,128)(2,1)} %get-tuple-element.68), channel_id=1, source_target_pairs={{0,128},{128,0},{1,129},{129,1},{2,130},{130,2},{3,131},{131,3},{4... | collective-permute-start | bytes 1572872 | tf_op jit(solution)/shard_map/ppermute | solution.py:322
  129.1 40.4 %collective-permute-start.15 = (bf16[512,512]{1,0:T(8,128)(2,1)}, bf16[512,512]{1,0:T(8,128)(2,1)}, u32[]{:S(2)}, u32[]{:S(2)}) collective-permute-start(bf16[512,512]{1,0:T(8,128)(2,1)} %get-tuple-element.69), channel_id=1, source_target_pairs={{0,136},{8,128},{128,8},{136,0},{1,137},{9,129},{129,9},{137,1},{2... | collective-permute-start | bytes 1572872 | tf_op jit(solution)/shard_map/ppermute | solution.py:323
  136.8 32.7 %collective-permute-start.16 = (bf16[512,512]{1,0:T(8,128)(2,1)}, bf16[512,512]{1,0:T(8,128)(2,1)}, u32[]{:S(2)}, u32[]{:S(2)}) collective-permute-start(bf16[512,512]{1,0:T(8,128)(2,1)} %broadcast_select_fusion.1), channel_id=1, source_target_pairs={{0,8},{8,0},{1,9},{9,1},{2,10},{10,2},{3,11},{11,3},{4,12},{12,4},... | collective-permute-start | bytes 1572872 | tf_op jit(solution)/shard_map/ppermute | solution.py:324
  150.1 22.2 %collective-permute-start.18 = (bf16[4,128,512]{2,1,0:T(8,128)(2,1)}, bf16[4,128,512]{2,1,0:T(8,128)(2,1)}, u32[]{:S(2)}, u32[]{:S(2)}) collective-permute-start(bf16[4,128,512]{2,1,0:T(8,128)(2,1)} %shard_map.176), channel_id=1, source_target_pairs={{0,128},{128,0},{1,129},{129,1},{2,130},{130,2},{3,131},{131,3},{4... | collective-permute-start | bytes 1572872 | tf_op jit(solution)/shard_map/ppermute | solution.py:365
  168.2 9.6 %collective-permute-start.17 = (bf16[512,256]{1,0:T(8,128)(2,1)S(1)}, bf16[512,256]{1,0:T(8,128)(2,1)}, u32[]{:S(2)}, u32[]{:S(2)}) collective-permute-start(bf16[512,256]{1,0:T(8,128)(2,1)S(1)} %slice_bitcast_fusion), channel_id=1, source_target_pairs={{0,128},{128,0},{1,129},{129,1},{2,130},{130,2},{3,131},{131,3},{4... | collective-permute-start | bytes 786440 | tf_op jit(solution)/shard_map/ppermute | solution.py:287
  (19 other events, 347.3 us)
Sparse Core Ops, SparseCore 0:
  27.4 62.6 all-gather.2
  108.2 58.9 reduce-scatter.1
